TPU v7x, 512 devices: a whole 4x4x16 slice. The times are simulated.
512 devices in a mesh: dp: 16 (over z), ctx: 16 (over x, y_lo, core), track: 2 (over y_hi).
Axes of the slice: x: 4, y: 4 (y_hi: 2, y_lo: 2; y = y_hi * 2 + y_lo), z: 16, core: 2. Of those that a mesh axis runs over, the one named last changes fastest.
Arguments:
- inputs: bfloat16 [16, 2048, 768], P('dp', 'ctx'), may hold values from -40 to 40
- teacher: bfloat16 [16, 2048, 2816], P('dp', 'ctx', 'track'), may hold values from -12 to 100
- member: int32 [16], P('dp'), may hold values from 0 to 3
- member_bias: float32 [4, 2816], P(None, 'track'), may hold values from -6 to 6
- assay: int32 [2816], P('track'), may hold values from 0 to 3
- assay_temp: float32 [4], replicated, may hold values from 0.25 to 1
- conv_weight: bfloat16 [2304, 384], P('dp'), may hold values from -0.125 to 0.125
- proj_weight: bfloat16 [384, 768], P('dp'), may hold values from -0.3125 to 0.3125
- head_weight: bfloat16 [768, 2816], P('dp', 'track')
Outputs:
- grad_input: float32 [16, 2048, 768], P('dp', 'ctx')
- grad_conv: float32 [2304, 384], P(('dp', 'ctx'))
All inputs are finite; a program needn't handle non-finite values.
Results may differ from a plain program's by a relative error of at most 0.0048.
Values may be sent and summed in bfloat16 or wider, within the bound.
No kernel may reach another device: no remote copies, remote signals or barrier semaphores. Data moves between devices by JAX's collectives and lax.ppermute only.
A program may use at most 64 MiB of HBM per device.

v0:
```python
import math

import jax
import jax.numpy as jnp
from jax import lax
from jax.sharding import PartitionSpec as P


def passed_along(value, axis, steps):
    count = lax.axis_size(axis)
    initial, last = (max(0, -steps), min(count, count - steps))
    return lax.ppermute(value, axis, [(source, source + steps) for source in range(initial, last)])


def gelu_tanh(values):
    return jax.nn.gelu(values, approximate=True)


def distant(values, offset):
    return passed_along(values, "ctx", offset)


def transposed_product(left, weight_rows):
    return lax.dot_general(
        left, weight_rows, (((1,), (1,)), ((), ())), preferred_element_type=jnp.float32
    )


def on_device(
    inputs, teacher, member, member_bias, assay, assay_temp, conv_weight, proj_weight, head_weight
):
    conv_full, proj_full, head_full = (
        lax.all_gather(conv_weight, "dp", axis=0, tiled=True),
        lax.all_gather(proj_weight, "dp", axis=0, tiled=True),
        lax.all_gather(head_weight, "dp", axis=0, tiled=True),
    )
    sequence_row_block = inputs[0]
    teacher_rows = teacher[0]
    pos_count = sequence_row_block.shape[0]
    width = sequence_row_block.shape[1]
    track_local = teacher_rows.shape[1]
    ctx_count = lax.axis_size("ctx")
    quarter = ctx_count // 4
    rows_before = distant(sequence_row_block, quarter)
    rows_after = distant(sequence_row_block, -quarter)
    stacked_taps = jnp.concatenate([rows_before, sequence_row_block, rows_after], axis=1)
    pre_act = jnp.dot(stacked_taps, conv_full, preferred_element_type=jnp.float32)
    gated = gelu_tanh(pre_act).astype(jnp.bfloat16)
    hidden = (
        sequence_row_block.astype(jnp.float32)
        + jnp.dot(gated, proj_full, preferred_element_type=jnp.float32)
    ).astype(jnp.bfloat16)
    student = jnp.dot(hidden, head_full, preferred_element_type=jnp.float32)
    member_hit = (jnp.arange(member_bias.shape[0], dtype=jnp.int32) == member[0]).astype(
        jnp.float32
    )
    member_row = jnp.sum(member_hit[:, None] * member_bias, axis=0)
    assay_hit = (
        assay[:, None] == jnp.arange(assay_temp.shape[0], dtype=jnp.int32)[None, :]
    ).astype(jnp.float32)
    temp_cols = jnp.sum(assay_hit * assay_temp[None, :], axis=1)
    target = (teacher_rows.astype(jnp.float32) + member_row[None, :]) / temp_cols[None, :]
    peak_student, peak_target = lax.pmax(
        (jnp.max(student, axis=1), jnp.max(target, axis=1)), "track"
    )
    total_student, total_target = lax.psum(
        (
            jnp.sum(jnp.exp(student - peak_student[:, None]), axis=1),
            jnp.sum(jnp.exp(target - peak_target[:, None]), axis=1),
        ),
        "track",
    )
    q_student = jnp.exp(student - peak_student[:, None]) / total_student[:, None]
    p_target = jnp.exp(target - peak_target[:, None]) / total_target[:, None]
    track_total = track_local * lax.axis_size("track")
    logit_grad = (track_total * (q_student - p_target)).astype(jnp.bfloat16)
    hidden_state_gradient = lax.psum(transposed_product(logit_grad, head_full), "track")
    hidden_grad_b = hidden_state_gradient.astype(jnp.bfloat16)
    gated_grad = transposed_product(hidden_grad_b, proj_full)
    unused, pullback = jax.vjp(gelu_tanh, pre_act)
    pre_grad = pullback(gated_grad)[0].astype(jnp.bfloat16)
    kernel_sum = lax.psum_scatter(
        lax.dot_general(
            stacked_taps, pre_grad, (((0,), (0,)), ((), ())), preferred_element_type=jnp.float32
        ),
        ("dp", "ctx"),
        scatter_dimension=0,
        tiled=True,
    )
    grad_conv = kernel_sum / math.sqrt(lax.axis_size("dp") * ctx_count * pos_count)
    grad_after = distant(pre_grad, -quarter)
    grad_before = distant(pre_grad, quarter)
    gradient_row_block = (
        hidden_state_gradient
        + transposed_product(grad_after, conv_full[0:width])
        + transposed_product(pre_grad, conv_full[width : 2 * width])
        + transposed_product(grad_before, conv_full[2 * width :])
    )
    return (gradient_row_block[None], grad_conv)


def solution(mesh):
    return jax.shard_map(
        on_device,
        mesh=mesh,
        in_specs=(
            P("dp", "ctx", None),
            P("dp", "ctx", "track"),
            P("dp"),
            P(None, "track"),
            P("track"),
            P(),
            P("dp", None),
            P("dp", None),
            P("dp", "track"),
        ),
        out_specs=(P("dp", "ctx", None), P(("dp", "ctx"), None)),
        check_vma=False,
    )
```

profile of v0, /device:TPU:1, one launch (start us, length us, event | category | flops | bytes accessed | tf_op | source)
XLA Modules:
  0.0 2358.1 jit_solution(13373687940790308962)
XLA Ops:
  8.7 1.3 collective-permute-start.1
  10.0 4.6 collective-permute-start
  15.2 0.8 multiply_reduce_fusion
  16.1 34.6 %all_gather.10 = bf16[384,768]{1,0:T(8,128)(2,1)S(1)} all-gather(bf16[24,768]{1,0:T(8,128)(2,1)} %param.16), channel_id=1, replica_groups=mesh['dp'=16,'ctx'=16,'track'=2] {'dp'}, dimensions={0}, use_global_device_ids=true | all-gather | bytes 626688 | tf_op jit(solution)/shard_map/all_gather | solution.py:34
  50.7 0.8 select_reduce_fusion
  51.5 1.2 fusion.27
  52.7 27.6 %all-gather.3.cloned.1.call-done = bf16[2304,384]{1,0:T(8,128)(2,1)} async-done(((bf16[144,384]{1,0:T(8,128)(2,1)}), bf16[2304,384]{1,0:T(8,128)(2,1)}) %all-gather.3.cloned.1.call-update) | async-done | bytes 1769488 | tf_op jit(solution)/shard_map/all_gather | solution.py:33
  80.3 2.7 fusion.14
  83.1 69.2 %all-gather.5.cloned.1.call-done = bf16[768,1408]{1,0:T(8,128)(2,1)} async-done(((bf16[48,1408]{1,0:T(8,128)(2,1)}), bf16[768,1408]{1,0:T(8,128)(2,1)}) %all-gather.5.cloned.1.call-update) | async-done | bytes 2162704 | tf_op jit(solution)/shard_map/all_gather | solution.py:35
  152.3 2.7 fusion.48
  155.0 5.3 all-reduce.2
  160.3 1.4 fusion.5
  161.7 5.4 all-reduce.1
  167.1 2.6 fusion.12
  169.8 57.0 %all-reduce.6.cloned.1.call-done = f32[128,768]{1,0:T(8,128)} async-done(((f32[128,768]{1,0:T(8,128)}), f32[128,768]{1,0:T(8,128)}) %all-reduce.6.cloned.1.call-update) | async-done | bytes 393232 | tf_op jit(solution)/shard_map/psum | solution.py:77
  226.8 1.4 fusion.21
  228.2 2.5 fusion.13
  230.7 1.4 dynamic-slice
  232.8 1.3 collective-permute-start.2
  234.1 4.0 collective-permute-start.3
  238.7 0.9 collective-permute-done.3
  239.7 1.1 fusion
  240.7 2109.4 %all-reduce.8.cloned.1.call-done = f32[2304,384]{1,0:T(8,128)} async-done(((f32[2304,384]{1,0:T(8,128)}), f32[2304,384]{1,0:T(8,128)}) %all-reduce.8.cloned.1.call-update) | async-done | bytes 3538960
  2350.2 1.4 dynamic-slice_multiply_fusion
  (30 shorter events, 2.2 us)
Async XLA Ops:
  7.2 73.2 %all-gather.3.cloned.1.call-start = ((), (), s32[]{:S(2)}) async-start(), calls=%async_computation | async-start | bytes 1880064 | tf_op jit(solution)/shard_map/all_gather | solution.py:33
  7.9 144.4 %all-gather.5.cloned.1.call-start = ((), (), s32[]{:S(2)}) async-start(), calls=%async_computation.1 | async-start | bytes 2297856 | tf_op jit(solution)/shard_map/all_gather | solution.py:35
  8.6 218.1 %all-reduce.6.cloned.1.call-start = ((), (), s32[]{:S(2)}) async-start(), calls=%async_computation.2 | async-start | bytes 786432 | tf_op jit(solution)/shard_map/psum | solution.py:77
  8.7 44.0 %collective-permute-start.1 = (bf16[128,768]{1,0:T(8,128)(2,1)}, bf16[128,768]{1,0:T(8,128)(2,1)S(1)}, u32[]{:S(2)}, u32[]{:S(2)}) collective-permute-start(bf16[128,768]{1,0:T(8,128)(2,1)} %bitcast.31), channel_id=1, source_target_pairs={{8,0},{10,2},{12,4},{14,6},{16,8},{18,10},{20,12},{22,14},{24,16},... | collective-permute-start | bytes 589832 | tf_op jit(solution)/shard_map/ppermute | solution.py:12
  10.0 42.7 %collective-permute-start = (bf16[128,768]{1,0:T(8,128)(2,1)}, bf16[128,768]{1,0:T(8,128)(2,1)S(1)}, u32[]{:S(2)}, u32[]{:S(2)}) collective-permute-start(bf16[128,768]{1,0:T(8,128)(2,1)} %bitcast.32), channel_id=1, source_target_pairs={{0,8},{2,10},{4,12},{6,14},{8,16},{10,18},{12,20},{14,22},{16,24},... | collective-permute-start | bytes 589832 | tf_op jit(solution)/shard_map/ppermute | solution.py:12
  52.6 30.4 %copy-start.4 = (bf16[128,768]{1,0:T(8,128)(2,1)}, bf16[128,768]{1,0:T(8,128)(2,1)S(1)}, u32[]{:S(2)}) copy-start(bf16[128,768]{1,0:T(8,128)(2,1)S(1)} %collective-permute-done.1) | copy-start | bytes 589828
  52.7 30.4 %copy-start.6 = (bf16[128,768]{1,0:T(8,128)(2,1)}, bf16[128,768]{1,0:T(8,128)(2,1)S(1)}, u32[]{:S(2)}) copy-start(bf16[128,768]{1,0:T(8,128)(2,1)S(1)} %collective-permute-done) | copy-start | bytes 589828
  152.3 14.8 copy-start
  169.7 58.5 %copy-start.2 = (bf16[1,128,768]{2,1,0:T(8,128)(2,1)S(1)}, bf16[1,128,768]{2,1,0:T(8,128)(2,1)}, u32[]{:S(2)}) copy-start(bf16[1,128,768]{2,1,0:T(8,128)(2,1)} %param.9) | copy-start | bytes 589828
  169.7 58.5 %copy-start.5 = (bf16[128,768]{1,0:T(8,128)(2,1)S(1)}, bf16[128,768]{1,0:T(8,128)(2,1)}, u32[]{:S(2)}) copy-start(bf16[128,768]{1,0:T(8,128)(2,1)} %copy-done.4) | copy-start | bytes 589828
  169.7 58.5 %copy-start.7 = (bf16[128,768]{1,0:T(8,128)(2,1)S(1)}, bf16[128,768]{1,0:T(8,128)(2,1)}, u32[]{:S(2)}) copy-start(bf16[128,768]{1,0:T(8,128)(2,1)} %copy-done.6) | copy-start | bytes 589828
  169.7 2180.5 %all-reduce.8.cloned.1.call-start = ((), (), s32[]{:S(2)}) async-start(), calls=%async_computation.3 | async-start | bytes 7077888
  230.7 7.4 copy-start.1
  230.7 7.7 copy-start.3
  232.8 5.6 collective-permute-start.2
  234.1 5.6 collective-permute-start.3
Sparse Core Ops, SparseCore 0:
  10.1 70.2 all-gather.2
  82.4 69.8 all-gather.4
  169.8 56.8 all-reduce.5
  230.8 2119.3 all-reduce.7
where the time goes:
time: 2360 us
  waiting for transfers between devices  2270 us (96%)
  blocking collectives  45.3 us (2%)
    unnamed x5, waiting for transfers between devices  2110 us
    all_gather x1, waiting for transfers between devices, on_device(): lax.all_gather(head_weight, 'dp', axis=0, tiled=True)  69.2 us
    psum x1, waiting for transfers between devices, on_device(): lax.psum(transposed_product(logit_grad, head_full), 'track')  57 us
  transfers between devices with their start and end apart: 8, of which 5 were waited for; matrix products, arithmetic and copies ran while one was open for 0% of the time, Pallas kernels for 0%

commit v1 on v0

v1 whole, which is shorter than its diff:
```python
import math

import jax
import jax.numpy as jnp
from jax import lax
from jax.sharding import Mesh, PartitionSpec as P

BF = jnp.bfloat16
F32 = jnp.float32
CTX = ("x", "yl", "c")
YR = ("yl", "yh")


def gelu_tanh(values):
    return jax.nn.gelu(values, approximate=True)


def spread(value, axis):
    count = lax.axis_size(axis)
    copies = jnp.broadcast_to(value[None], (count,) + value.shape)
    return lax.all_to_all(copies, axis, 0, 0)


def shifted(value, steps):
    count = lax.axis_size("x")
    first, last = max(0, -steps), min(count, count - steps)
    return lax.ppermute(value, "x", [(s, s + steps) for s in range(first, last)])


def swapped(value, axis):
    return lax.ppermute(value, axis, [(0, 1), (1, 0)])


def rows_product(left, weight_rows):
    return lax.dot_general(
        left, weight_rows, (((1,), (1,)), ((), ())), preferred_element_type=F32
    )


def on_device(
    inputs, teacher, member, member_bias, assay, assay_temp, conv_weight, proj_weight, head_weight
):
    rows = inputs[0]
    pos, width = rows.shape
    half = pos // 2
    ch = conv_weight.shape[1]
    zc = lax.axis_size("z")
    cc = lax.axis_size(CTX)
    yh = lax.axis_index("yh")

    head_full = lax.all_gather(head_weight, "z", axis=0, tiled=True)

    rows_before = shifted(rows, 1)
    rows_after = shifted(rows, -1)

    proj_cut = proj_weight.shape[0]
    packed = jnp.concatenate([conv_weight, proj_weight[:, :ch], proj_weight[:, ch:]], axis=0)
    slab = packed.shape[0] // 8
    place = lax.axis_index(("c", "yl", "yh"))
    mine = lax.dynamic_slice_in_dim(packed, place * slab, slab, axis=0)
    over_z = spread(mine, "z")
    over_y = spread(over_z, YR).reshape(4, zc, slab, ch)
    other = swapped(over_y, "c")
    core = lax.axis_index("c")
    first = jnp.where(core == 0, over_y, other)
    second = jnp.where(core == 0, other, over_y)
    slabs = jnp.concatenate([first, second], axis=0)
    conv_slabs = conv_weight.shape[0] // slab
    conv_full = slabs[:conv_slabs].transpose(1, 0, 2, 3).reshape(zc * conv_weight.shape[0], ch)
    proj_left = slabs[conv_slabs].reshape(zc * proj_cut, ch)
    proj_right = slabs[conv_slabs + 1].reshape(zc * proj_cut, ch)
    proj_full = jnp.concatenate([proj_left, proj_right], axis=1)

    member_hit = (jnp.arange(member_bias.shape[0], dtype=jnp.int32) == member[0]).astype(F32)
    member_row = jnp.sum(member_hit[:, None] * member_bias, axis=0)
    assay_hit = (
        assay[:, None] == jnp.arange(assay_temp.shape[0], dtype=jnp.int32)[None, :]
    ).astype(F32)
    temp_cols = jnp.sum(assay_hit * assay_temp[None, :], axis=1)
    target = (teacher[0].astype(F32) + member_row[None, :]) / temp_cols[None, :]
    peak_t = jnp.max(target, axis=1)
    exp_t = jnp.exp(target - peak_t[:, None])
    sum_t = jnp.sum(exp_t, axis=1)

    stacked = jnp.concatenate([rows_before, rows, rows_after], axis=1)
    pre_act = jnp.dot(stacked, conv_full, preferred_element_type=F32)
    gated = gelu_tanh(pre_act).astype(BF)
    hidden = (rows.astype(F32) + jnp.dot(gated, proj_full, preferred_element_type=F32)).astype(BF)

    part = conv_weight.shape[0] // cc
    by_owner = stacked.T.reshape(zc, cc, part, pos).transpose(1, 0, 2, 3).reshape(cc, zc * part, pos)
    owned = lax.all_to_all(by_owner, CTX, 0, 0)
    owned = lax.dynamic_slice_in_dim(owned, yh * half, half, axis=2)
    owned = owned.transpose(1, 0, 2).reshape(zc * part, cc * half)

    student = jnp.dot(hidden, head_full, preferred_element_type=F32)
    peak_s = jnp.max(student, axis=1)
    exp_s = jnp.exp(student - peak_s[:, None])
    sum_s = jnp.sum(exp_s, axis=1)
    stats = lax.all_gather(jnp.stack([peak_s, sum_s, peak_t, sum_t]), "yh", axis=0)
    top_s = jnp.maximum(stats[0, 0], stats[1, 0])
    top_t = jnp.maximum(stats[0, 2], stats[1, 2])
    total_s = stats[0, 1] * jnp.exp(stats[0, 0] - top_s) + stats[1, 1] * jnp.exp(stats[1, 0] - top_s)
    total_t = stats[0, 3] * jnp.exp(stats[0, 2] - top_t) + stats[1, 3] * jnp.exp(stats[1, 2] - top_t)
    tracks = teacher.shape[2] * lax.axis_size("yh")
    scale_s = tracks * jnp.exp(peak_s - top_s) / total_s
    scale_t = tracks * jnp.exp(peak_t - top_t) / total_t
    logit_grad = (exp_s * scale_s[:, None] - exp_t * scale_t[:, None]).astype(BF)
    partial = rows_product(logit_grad, head_full)

    sent = lax.dynamic_slice_in_dim(partial, (1 - yh) * half, half, axis=0).astype(BF)
    kept = lax.dynamic_slice_in_dim(partial, yh * half, half, axis=0)
    hidden_grad = kept + swapped(sent, "yh").astype(F32)
    gated_grad = rows_product(hidden_grad.astype(BF), proj_full)
    unused, pullback = jax.vjp(gelu_tanh, lax.dynamic_slice_in_dim(pre_act, yh * half, half, axis=0))
    pre_grad = pullback(gated_grad)[0].astype(BF)

    grad_after = shifted(pre_grad, -1)
    grad_before = shifted(pre_grad, 1)
    everyone = lax.all_gather(pre_grad, CTX, axis=0, tiled=True)
    kernel_part = jnp.dot(owned, everyone, preferred_element_type=F32).astype(BF)
    kernel_part = kernel_part.reshape(zc, 1, part, ch)
    kernel_part = jnp.broadcast_to(kernel_part, (zc, 2, part, ch)).reshape(2 * zc, part, ch)
    terms = lax.all_to_all(kernel_part, ("z", "yh"), 0, 0)
    grad_conv = jnp.sum(terms.astype(F32), axis=0) / math.sqrt(zc * cc * pos)

    grad_rows = (
        hidden_grad
        + rows_product(grad_after, conv_full[:width])
        + rows_product(pre_grad, conv_full[width : 2 * width])
        + rows_product(grad_before, conv_full[2 * width :])
    )
    grad_other = swapped(grad_rows, "yh")
    grad_input = jnp.where(
        yh == 0,
        jnp.concatenate([grad_rows, grad_other], axis=0),
        jnp.concatenate([grad_other, grad_rows], axis=0),
    )
    return (grad_input[None], grad_conv)


def solution(mesh):
    fine = Mesh(mesh.devices.reshape(16, 4, 2, 2, 2), ("z", "x", "yl", "c", "yh"))
    return jax.shard_map(
        on_device,
        mesh=fine,
        in_specs=(
            P("z", CTX, None),
            P("z", CTX, "yh"),
            P("z"),
            P(None, "yh"),
            P("yh"),
            P(),
            P("z", None),
            P("z", None),
            P("z", "yh"),
        ),
        out_specs=(P("z", CTX, None), P(("z",) + CTX, None)),
        check_vma=False,
    )
```

time: 2360 us -> 195 us (0.08)
  the two profiles are of different devices: /device:TPU:1 before, /device:TPU:16 now
where the time goes in v1:
time: 195 us; the launch traced here: 194 us
  waiting for transfers between devices  70 us (36%)
  starting transfers between devices  44.3 us (23%)
  blocking collectives  41 us (21%)
  between operations  15.1 us (8%)
  matrix products  9.83 us (5%)
  local copies, waits for them, and re-layouts  8.65 us (4%)
  other arithmetic  4.86 us (2%)
    all_gather x1, blocking collectives, on_device(): everyone = lax.all_gather(pre_grad, CTX, axis=0, tiled=True)  21.2 us
    all_to_all x1, waiting for transfers between devices, spread(): return lax.all_to_all(copies, axis, 0, 0)  18.5 us
    all_gather x1, waiting for transfers between devices, on_device(): head_full = lax.all_gather(head_weight, 'z', axis=0, tiled=True)  17.8 us
    all_to_all x1, starting transfers between devices, spread(): return lax.all_to_all(copies, axis, 0, 0)  15.2 us
    all_to_all x1, blocking collectives, spread(): return lax.all_to_all(copies, axis, 0, 0)  13.8 us
    ppermute x3, waiting for transfers between devices, swapped(): return lax.ppermute(value, axis, [(0, 1), (1, 0)])  13.6 us
    all_to_all x1, starting transfers between devices, on_device(): terms = lax.all_to_all(kernel_part, ('z', 'yh'), 0, 0)  10.8 us
    ppermute x4, waiting for transfers between devices, shifted(): lax.ppermute(value, 'x', [(s, s + steps) for s in range(first, last)])  10.6 us
  transfers between devices with their start and end apart: 11, of which 8 were waited for; matrix products, arithmetic and copies ran while one was open for 9% of the time, Pallas kernels for 0%

profile of v1, /device:TPU:16, one launch (start us, length us, event | category | flops | bytes accessed | tf_op | source)
XLA Modules:
  0.0 193.7 jit_solution(13638966694532813308)
XLA Ops:
  9.4 15.2 %all-to-all-start = ((bf16[16,24,384]{2,1,0:T(8,128)(2,1)}), bf16[16,24,384]{2,1,0:T(8,128)(2,1)S(1)}, u32[]{:S(2)}, u32[]{:S(2)}) async-start(bf16[16,24,384]{2,1,0:T(8,128)(2,1)} %broadcast_in_dim.8), calls=%async_computation | async-start | bytes 589824 | tf_op jit(solution)/shard_map/all_to_all | solution.py:21
  25.4 18.5 %all-to-all-done = bf16[16,24,384]{2,1,0:T(8,128)(2,1)S(1)} async-done(((bf16[16,24,384]{2,1,0:T(8,128)(2,1)}), bf16[16,24,384]{2,1,0:T(8,128)(2,1)S(1)}, u32[]{:S(2)}, u32[]{:S(2)}) %all-to-all-start) | async-done | bytes 294944 | tf_op jit(solution)/shard_map/all_to_all | solution.py:21
  44.0 13.8 %all_to_all.20 = bf16[4,16,24,384]{3,2,1,0:T(8,128)(2,1)S(1)} all-to-all(bf16[4,16,24,384]{3,2,1,0:T(8,128)(2,1)S(1)} %broadcast_in_dim.9), channel_id=1, replica_groups=mesh['z'=16,'x'=4,'yl'=2,'c'=2,'yh'=2] {'yl','yh'}, dimensions={0} | all-to-all | bytes 2359296 | tf_op jit(solution)/shard_map/all_to_all | solution.py:21
  59.0 1.9 collective-permute-start.2
  60.9 3.4 %collective-permute-start = (bf16[128,768]{1,0:T(8,128)(2,1)S(1)}, bf16[128,768]{1,0:T(8,128)(2,1)S(1)}, u32[]{:S(2)}, u32[]{:S(2)}) collective-permute-start(bf16[128,768]{1,0:T(8,128)(2,1)S(1)} %bitcast.101), channel_id=1, source_target_pairs={{0,8},{8,16},{16,24},{1,9},{9,17},{17,25},{2,10},{10,18},{18,26},{... | collective-permute-start | bytes 589832 | tf_op jit(solution)/shard_map/ppermute | solution.py:27
  64.3 1.3 collective-permute-start.1
  67.0 2.1 %collective-permute-done = bf16[128,768]{1,0:T(8,128)(2,1)S(1)} collective-permute-done((bf16[128,768]{1,0:T(8,128)(2,1)S(1)}, bf16[128,768]{1,0:T(8,128)(2,1)S(1)}, u32[]{:S(2)}, u32[]{:S(2)}) %collective-permute-start) | collective-permute-done | bytes 196640 | tf_op jit(solution)/shard_map/ppermute | solution.py:27
  69.1 4.1 %collective-permute-done.1 = bf16[128,768]{1,0:T(8,128)(2,1)S(1)} collective-permute-done((bf16[128,768]{1,0:T(8,128)(2,1)S(1)}, bf16[128,768]{1,0:T(8,128)(2,1)S(1)}, u32[]{:S(2)}, u32[]{:S(2)}) %collective-permute-start.1) | collective-permute-done | bytes 196640 | tf_op jit(solution)/shard_map/ppermute | solution.py:27
  75.6 4.6 %all-to-all-start.2 = ((bf16[16,144,128]{2,1,0:T(8,128)(2,1)}), bf16[16,144,128]{2,1,0:T(8,128)(2,1)S(1)}, u32[]{:S(2)}, u32[]{:S(2)}) async-start(bf16[16,144,128]{2,1,0:T(8,128)(2,1)} %copy.41), calls=%async_computation.2 | async-start | bytes 1179648 | tf_op jit(solution)/shard_map/all_to_all | solution.py:92
  80.3 1.5 broadcast_select_fusion.1
  84.4 17.8 %all-gather.4.cloned.1.call-done = bf16[768,1408]{1,0:T(8,128)(2,1)} async-done(((bf16[48,1408]{1,0:T(8,128)(2,1)}), bf16[768,1408]{1,0:T(8,128)(2,1)}) %all-gather.4.cloned.1.call-update) | async-done | bytes 2162704 | tf_op jit(solution)/shard_map/all_gather | solution.py:51
  102.2 2.8 %fusion.80 = (f32[128]{0:T(128)S(1)}, f32[128,1408]{1,0:T(8,128)S(1)}) fusion(bf16[768,1408]{1,0:T(8,128)(2,1)} %all-gather.4.cloned.1.call-done, bf16[384,384]{1,0:T(8,128)(2,1)} %bitcast.99, bf16[384,384]{1,0:T(8,128)(2,1)} %bitcast.97, f32[128,384]{1,0:T(8,128)} %fusion.20, bf16[1,128,768]{2,1,0:T(8,128)(2,1)} %param.9), kind=kOutput, calls=%fused_computation.104 | convolution fusion | flops 354418560 | bytes 3867136 | tf_op jit(solution)/shard_map/dot_general | solution.py:96
  105.2 5.9 %all-gather.1 = f32[2,4,128]{2,1,0:T(4,128)S(1)} all-gather(f32[1,4,128]{2,1,0:T(4,128)S(1)} %maximum_bitcast_fusion), channel_id=2, replica_groups=mesh['z'=16,'x'=4,'yl'=2,'c'=2,'yh'=2] {'yh'}, dimensions={0}, use_global_device_ids=true | all-gather | bytes 6144 | tf_op jit(solution)/shard_map/all_gather | solution.py:100
  111.1 2.4 %fusion.14 = f32[128,768]{1,0:T(8,128)S(1)} fusion(bf16[768,1408]{1,0:T(8,128)(2,1)} %all-gather.4.cloned.1.call-done, f32[128,1408]{1,0:T(8,128)S(1)} %get-tuple-element.11, f32[128]{0:T(128)S(1)} %get-tuple-element.9, f32[128]{0:T(128)S(1)} %get-tuple-element.8, f32[128]{0:T(128)S(1)} %fusion.30, f32[128]{0:T(128)S(1)} %get-tuple-element.10, ...), kind=kOutput, calls=%fused_computation.29 | convolution fusion | flops 278446080 | bytes 3650560 | tf_op jit(solution)/shard_map/dot_general | solution.py:35
  114.3 2.3 %collective-permute-start.3 = (bf16[64,768]{1,0:T(8,128)(2,1)}, bf16[64,768]{1,0:T(8,128)(2,1)}, u32[]{:S(2)}, u32[]{:S(2)}) collective-permute-start(bf16[64,768]{1,0:T(8,128)(2,1)} %dynamic-slice_convert_fusion), channel_id=1, source_target_pairs={{0,1},{1,0},{2,3},{3,2},{4,5},{5,4},{6,7},{7,6},{8,9},{9,8},{10,11... | collective-permute-start | bytes 294920 | tf_op jit(solution)/shard_map/ppermute | solution.py:31
  117.4 5.2 %collective-permute-done.3 = bf16[64,768]{1,0:T(8,128)(2,1)} collective-permute-done((bf16[64,768]{1,0:T(8,128)(2,1)}, bf16[64,768]{1,0:T(8,128)(2,1)}, u32[]{:S(2)}, u32[]{:S(2)}) %collective-permute-start.3) | collective-permute-done | bytes 98336 | tf_op jit(solution)/shard_map/ppermute | solution.py:31
  122.7 1.3 fusion.39
  124.0 21.2 %all_gather.15 = bf16[1024,384]{1,0:T(8,128)(2,1)S(1)} all-gather(bf16[64,384]{1,0:T(8,128)(2,1)S(1)} %fusion.39), channel_id=1, replica_groups=mesh['z'=16,'x'=4,'yl'=2,'c'=2,'yh'=2] {'x','yl','c'}, dimensions={0}, use_global_device_ids=true | all-gather | bytes 835584 | tf_op jit(solution)/shard_map/all_gather | solution.py:120
  147.7 10.8 %all-to-all-start.3 = ((bf16[32,9,384]{2,1,0:T(8,128)(2,1)}), bf16[32,9,384]{2,1,0:T(8,128)(2,1)S(1)}, u32[]{:S(2)}, u32[]{:S(2)}) async-start(bf16[32,9,384]{2,1,0:T(8,128)(2,1)} %bitcast.27), calls=%async_computation.3 | async-start | bytes 786432 | tf_op jit(solution)/shard_map/all_to_all | solution.py:124
  158.8 1.3 collective-permute-start.4
  160.5 4.4 %collective-permute-done.4 = bf16[64,384]{1,0:T(8,128)(2,1)S(1)} collective-permute-done((bf16[64,384]{1,0:T(8,128)(2,1)S(1)}, bf16[64,384]{1,0:T(8,128)(2,1)S(1)}, u32[]{:S(2)}, u32[]{:S(2)}) %collective-permute-start.4) | collective-permute-done | bytes 49184 | tf_op jit(solution)/shard_map/ppermute | solution.py:27
  166.0 2.1 %collective-permute-start.6 = (f32[64,768]{1,0:T(8,128)S(1)}, f32[64,768]{1,0:T(8,128)S(1)}, u32[]{:S(2)}, u32[]{:S(2)}) collective-permute-start(f32[64,768]{1,0:T(8,128)S(1)} %fusion.2), channel_id=1, source_target_pairs={{0,1},{1,0},{2,3},{3,2},{4,5},{5,4},{6,7},{7,6},{8,9},{9,8},{10,11... | collective-permute-start | bytes 589832 | tf_op jit(solution)/shard_map/ppermute | solution.py:31
  168.2 8.4 %collective-permute-done.6 = f32[64,768]{1,0:T(8,128)S(1)} collective-permute-done((f32[64,768]{1,0:T(8,128)S(1)}, f32[64,768]{1,0:T(8,128)S(1)}, u32[]{:S(2)}, u32[]{:S(2)}) %collective-permute-start.6) | collective-permute-done | bytes 196640 | tf_op jit(solution)/shard_map/ppermute | solution.py:31
  177.4 8.8 %all-to-all-done.3 = bf16[32,9,384]{2,1,0:T(8,128)(2,1)S(1)} async-done(((bf16[32,9,384]{2,1,0:T(8,128)(2,1)}), bf16[32,9,384]{2,1,0:T(8,128)(2,1)S(1)}, u32[]{:S(2)}, u32[]{:S(2)}) %all-to-all-start.3) | async-done | bytes 221216 | tf_op jit(solution)/shard_map/all_to_all | solution.py:124
  (68 shorter events, 17.3 us)
Async XLA Ops:
  9.4 34.5 %all-to-all-start = ((bf16[16,24,384]{2,1,0:T(8,128)(2,1)}), bf16[16,24,384]{2,1,0:T(8,128)(2,1)S(1)}, u32[]{:S(2)}, u32[]{:S(2)}) async-start(bf16[16,24,384]{2,1,0:T(8,128)(2,1)} %broadcast_in_dim.8), calls=%async_computation | async-start | bytes 589824 | tf_op jit(solution)/shard_map/all_to_all | solution.py:21
  24.6 77.6 %all-gather.4.cloned.1.call-start = ((), (), s32[]{:S(2)}) async-start(), calls=%async_computation.4 | async-start | bytes 2297856 | tf_op jit(solution)/shard_map/all_gather | solution.py:51
  57.8 3.1 %copy-start.3 = (bf16[1,128,768]{2,1,0:T(8,128)(2,1)S(1)}, bf16[1,128,768]{2,1,0:T(8,128)(2,1)}, u32[]{:S(2)}) copy-start(bf16[1,128,768]{2,1,0:T(8,128)(2,1)} %param.9) | copy-start | bytes 589828
  57.8 8.5 %copy-start.12 = (s32[1408]{0:T(1024)S(1)}, s32[1408]{0:T(1024)}, u32[]{:S(2)}) copy-start(s32[1408]{0:T(1024)} %param.13) | copy-start | bytes 16900
  57.8 8.5 %copy-start.13 = (f32[4]{0:T(128)S(1)}, f32[4]{0:T(128)}, u32[]{:S(2)}) copy-start(f32[4]{0:T(128)} %param.14) | copy-start | bytes 52
  57.8 8.6 %copy-start.11 = (f32[4,1408]{1,0:T(4,128)S(1)}, f32[4,1408]{1,0:T(4,128)}, u32[]{:S(2)}) copy-start(f32[4,1408]{1,0:T(4,128)} %param.12) | copy-start | bytes 67588
  57.8 8.7 %copy-start = (bf16[1,128,1408]{2,1,0:T(8,128)(2,1)S(1)}, bf16[1,128,1408]{2,1,0:T(8,128)(2,1)}, u32[]{:S(2)}) copy-start(bf16[1,128,1408]{2,1,0:T(8,128)(2,1)} %param.10) | copy-start | bytes 1081348
  59.0 21.3 %collective-permute-start.2 = (bf16[4,16,24,384]{3,2,0,1:T(8,128)(2,1)}, bf16[4,16,24,384]{3,2,0,1:T(8,128)(2,1)}, u32[]{:S(2)}, u32[]{:S(2)}) collective-permute-start(bf16[4,16,24,384]{3,2,0,1:T(8,128)(2,1)} %copy.37), channel_id=1, source_target_pairs={{0,2},{2,0},{1,3},{3,1},{4,6},{6,4},{5,7},{7,5},{8,10},{10,8},{9,1... | collective-permute-start | bytes 3538952 | tf_op jit(solution)/shard_map/ppermute | solution.py:31
  60.9 8.2 %collective-permute-start = (bf16[128,768]{1,0:T(8,128)(2,1)S(1)}, bf16[128,768]{1,0:T(8,128)(2,1)S(1)}, u32[]{:S(2)}, u32[]{:S(2)}) collective-permute-start(bf16[128,768]{1,0:T(8,128)(2,1)S(1)} %bitcast.101), channel_id=1, source_target_pairs={{0,8},{8,16},{16,24},{1,9},{9,17},{17,25},{2,10},{10,18},{18,26},{... | collective-permute-start | bytes 589832 | tf_op jit(solution)/shard_map/ppermute | solution.py:27
  64.3 8.9 %collective-permute-start.1 = (bf16[128,768]{1,0:T(8,128)(2,1)S(1)}, bf16[128,768]{1,0:T(8,128)(2,1)S(1)}, u32[]{:S(2)}, u32[]{:S(2)}) collective-permute-start(bf16[128,768]{1,0:T(8,128)(2,1)S(1)} %bitcast.102), channel_id=1, source_target_pairs={{8,0},{16,8},{24,16},{9,1},{17,9},{25,17},{10,2},{18,10},{26,18},{... | collective-permute-start | bytes 589832 | tf_op jit(solution)/shard_map/ppermute | solution.py:27
  69.1 4.2 %copy-start.7 = (bf16[128,768]{1,0:T(8,128)(2,1)}, bf16[128,768]{1,0:T(8,128)(2,1)S(1)}, u32[]{:S(2)}) copy-start(bf16[128,768]{1,0:T(8,128)(2,1)S(1)} %collective-permute-done) | copy-start | bytes 589828
  75.6 41.0 %all-to-all-start.2 = ((bf16[16,144,128]{2,1,0:T(8,128)(2,1)}), bf16[16,144,128]{2,1,0:T(8,128)(2,1)S(1)}, u32[]{:S(2)}, u32[]{:S(2)}) async-start(bf16[16,144,128]{2,1,0:T(8,128)(2,1)} %copy.41), calls=%async_computation.2 | async-start | bytes 1179648 | tf_op jit(solution)/shard_map/all_to_all | solution.py:92
  82.0 0.9 copy-start.8
  82.0 1.2 copy-start.10
  113.5 0.8 copy-start.4
  114.3 8.3 %collective-permute-start.3 = (bf16[64,768]{1,0:T(8,128)(2,1)}, bf16[64,768]{1,0:T(8,128)(2,1)}, u32[]{:S(2)}, u32[]{:S(2)}) collective-permute-start(bf16[64,768]{1,0:T(8,128)(2,1)} %dynamic-slice_convert_fusion), channel_id=1, source_target_pairs={{0,1},{1,0},{2,3},{3,2},{4,5},{5,4},{6,7},{7,6},{8,9},{9,8},{10,11... | collective-permute-start | bytes 294920 | tf_op jit(solution)/shard_map/ppermute | solution.py:31
  116.8 5.8 %copy-start.1 = (bf16[1,16,24,384]{3,2,0,1:T(8,128)(2,1)S(1)}, bf16[1,16,24,384]{3,2,0,1:T(8,128)(2,1)}, u32[]{:S(2)}) copy-start(bf16[1,16,24,384]{3,2,0,1:T(8,128)(2,1)} %get-tuple-element.4) | copy-start | bytes 884740
  116.8 5.8 %copy-start.2 = (bf16[1,16,24,384]{3,2,0,1:T(8,128)(2,1)S(1)}, bf16[1,16,24,384]{3,2,0,1:T(8,128)(2,1)}, u32[]{:S(2)}) copy-start(bf16[1,16,24,384]{3,2,0,1:T(8,128)(2,1)} %get-tuple-element.5) | copy-start | bytes 884740
  116.9 5.8 %copy-start.6 = (f32[128,384]{1,0:T(8,128)S(1)}, f32[128,384]{1,0:T(8,128)}, u32[]{:S(2)}) copy-start(f32[128,384]{1,0:T(8,128)} %fusion.20) | copy-start | bytes 589828
  145.2 14.9 %collective-permute-start.5 = (bf16[64,384]{1,0:T(8,128)(2,1)S(1)}, bf16[64,384]{1,0:T(8,128)(2,1)S(1)}, u32[]{:S(2)}, u32[]{:S(2)}) collective-permute-start(bf16[64,384]{1,0:T(8,128)(2,1)S(1)} %fusion.39), channel_id=1, source_target_pairs={{0,8},{8,16},{16,24},{1,9},{9,17},{17,25},{2,10},{10,18},{18,26},{... | collective-permute-start | bytes 147464 | tf_op jit(solution)/shard_map/ppermute | solution.py:27
  147.7 17.1 %copy-start.5 = (f32[128,768]{1,0:T(8,128)S(1)}, f32[128,768]{1,0:T(8,128)}, u32[]{:S(2)}) copy-start(f32[128,768]{1,0:T(8,128)} %copy-done.4) | copy-start | bytes 1179652
  147.7 38.5 %all-to-all-start.3 = ((bf16[32,9,384]{2,1,0:T(8,128)(2,1)}), bf16[32,9,384]{2,1,0:T(8,128)(2,1)S(1)}, u32[]{:S(2)}, u32[]{:S(2)}) async-start(bf16[32,9,384]{2,1,0:T(8,128)(2,1)} %bitcast.27), calls=%async_computation.3 | async-start | bytes 786432 | tf_op jit(solution)/shard_map/all_to_all | solution.py:124
  158.8 6.0 %collective-permute-start.4 = (bf16[64,384]{1,0:T(8,128)(2,1)S(1)}, bf16[64,384]{1,0:T(8,128)(2,1)S(1)}, u32[]{:S(2)}, u32[]{:S(2)}) collective-permute-start(bf16[64,384]{1,0:T(8,128)(2,1)S(1)} %fusion.39), channel_id=1, source_target_pairs={{8,0},{16,8},{24,16},{9,1},{17,9},{25,17},{10,2},{18,10},{26,18},{... | collective-permute-start | bytes 147464 | tf_op jit(solution)/shard_map/ppermute | solution.py:27
  166.0 10.5 %collective-permute-start.6 = (f32[64,768]{1,0:T(8,128)S(1)}, f32[64,768]{1,0:T(8,128)S(1)}, u32[]{:S(2)}, u32[]{:S(2)}) collective-permute-start(f32[64,768]{1,0:T(8,128)S(1)} %fusion.2), channel_id=1, source_target_pairs={{0,1},{1,0},{2,3},{3,2},{4,5},{5,4},{6,7},{7,6},{8,9},{9,8},{10,11... | collective-permute-start | bytes 589832 | tf_op jit(solution)/shard_map/ppermute | solution.py:31
  (1 other events, 0.7 us)
Sparse Core Ops, SparseCore 0:
  27.5 74.5 all-gather.3

commit v2 on v1

v2 whole, which is shorter than its diff:
```python
import functools
import math

import jax
import jax.numpy as jnp
from jax import lax
from jax.experimental import pallas as pl
from jax.experimental.pallas import tpu as pltpu
from jax.sharding import Mesh, PartitionSpec as P

BF = jnp.bfloat16
F32 = jnp.float32
CTX = ("x", "yl", "c")
YR = ("yl", "yh")
VMEM_LIMIT = 12
CURVE = 0.044715
SLOPE = math.sqrt(2.0 / math.pi)
SDS = jax.ShapeDtypeStruct


def gelu_tanh(values):
    return 0.5 * values * (1.0 + jnp.tanh(SLOPE * (values + CURVE * values * values * values)))


def gelu_slope(values):
    square = values * values
    bend = jnp.tanh(SLOPE * (values + CURVE * values * square))
    return 0.5 * (1.0 + bend) + 0.5 * values * (1.0 - bend * bend) * SLOPE * (
        1.0 + 3.0 * CURVE * square
    )


def mm(left, right):
    return jnp.dot(left, right, preferred_element_type=F32)


def mm_t(left, right_rows):
    return lax.dot_general(
        left, right_rows, (((1,), (1,)), ((), ())), preferred_element_type=F32
    )


def shifted(value, steps):
    count = lax.axis_size("x")
    first, last = max(0, -steps), min(count, count - steps)
    return lax.ppermute(value, "x", [(s, s + steps) for s in range(first, last)])


def swapped(value, axis):
    return lax.ppermute(value, axis, [(0, 1), (1, 0)])


def call(body, outs, scratch, flops, moved, scalar, *args, far=(), far_out=(), limit=VMEM_LIMIT):
    def spec(k, distant):
        return pl.BlockSpec(memory_space=pltpu.HBM if k in distant else pltpu.VMEM)

    specs = [spec(k, far) for k in range(len(args))]
    if scalar is not None:
        specs = [pl.BlockSpec(memory_space=pltpu.SMEM)] + specs
        args = (scalar,) + args
    return pl.pallas_call(
        body,
        out_shape=outs,
        in_specs=specs,
        out_specs=[spec(k, far_out) for k in range(len(outs))],
        scratch_shapes=scratch,
        compiler_params=pltpu.CompilerParams(vmem_limit_bytes=limit * 1024 * 1024),
        cost_estimate=pl.CostEstimate(flops=flops, bytes_accessed=moved, transcendentals=0),
    )(*args)


def pack_kernel(place, conv_far, proj_far, head_far, out, conv, proj, head, conv_wide, head_wide, sems):
    core, y, x = place[0], place[1], place[2]
    loads = [
        pltpu.make_async_copy(far, near, sems.at[k])
        for k, (far, near) in enumerate(((proj_far, proj), (conv_far, conv), (head_far, head)))
    ]
    for load in loads:
        load.start()
    granule, ch = out.shape[1], out.shape[2]
    tracks = head.shape[1]
    head_wide[:, tracks:] = jnp.zeros((head.shape[0], head_wide.shape[1] - tracks), F32)
    source = lax.broadcasted_iota(jnp.int32, (proj.shape[1], ch), 0)
    target = lax.broadcasted_iota(jnp.int32, (proj.shape[1], ch), 1)
    block = jnp.floor((target.astype(F32) + 0.5) * (1.0 / granule)).astype(jnp.int32)
    picked = (source == target + granule * block + granule * core).astype(F32).astype(BF)
    loads[0].wait()
    low = mm(proj[...], picked)
    loads[1].wait()
    conv_wide[...] = conv[...].astype(F32)
    loads[2].wait()
    head_wide[:, :tracks] = head[...].astype(F32)
    deep = conv.shape[0] // 2
    at = pl.multiple_of(core * deep + jnp.minimum(y, 2) * granule, 8)
    out[0] = jnp.where(y < 3, conv_wide[pl.ds(at, granule), :], low).astype(BF)
    out[1] = head_wide[
        pl.ds(pl.multiple_of(core * granule, 8), granule), pl.ds(pl.multiple_of(x * ch, 128), ch)
    ].astype(BF)


def copies_kernel(gathered, out):
    for k in range(out.shape[0]):
        out[k] = gathered[:, 0]


def prepare_kernel(
    core_ref, before, rows, following, gathered, early, taps_far, in_far, owner_far, head_far,
    tall, sorted_, kinds, owners, taps, ins, by_owner, sems
):
    stores = [
        pltpu.make_async_copy(gathered.at[:, 1], head_far.at[k], sems.at[k])
        for k in range(head_far.shape[0])
    ]
    for store in stores:
        store.start()
    core = core_ref[0]
    pos, width = rows.shape
    for at, source in enumerate((before, rows, following)):
        tall[at * width : (at + 1) * width, :] = jnp.transpose(source[...].astype(F32))
    count, granule = 16, 24
    deep = taps.shape[2]
    cut = 2 * deep // count
    for c in range(2):
        for y in range(3):
            for z in range(count):
                source = z * cut + c * (cut // 2) + y * granule
                target = (y * count + z) * granule
                sorted_[c, target : target + granule, :] = tall[source : source + granule, :]
        for z in range(count):
            source = width + (2 * z + c) * granule
            kinds[c, z * granule : (z + 1) * granule, :] = tall[source : source + granule, :]
    for k, at in enumerate((core, 1 - core)):
        taps[k] = jnp.transpose(sorted_[at]).astype(BF)
        ins[k] = jnp.transpose(kinds[at]).astype(BF)
    stores.append(pltpu.make_async_copy(taps, taps_far, sems.at[4]))
    stores.append(pltpu.make_async_copy(ins, in_far, sems.at[5]))
    for store in stores[4:]:
        store.start()
    owner_count = by_owner.shape[0]
    part = cut // owner_count
    for k in range(owner_count):
        for z in range(count):
            owners[k, z * part : (z + 1) * part, :] = tall[z * cut + k * part : z * cut + (k + 1) * part, :]
        by_owner[k] = owners[k].astype(BF)
    stores.append(pltpu.make_async_copy(by_owner, owner_far, sems.at[6]))
    stores[6].start()
    for store in stores:
        store.wait()


def conv_kernel(
    taps, ins, own, other, pre_ref, hid_own, hid_other
):
    ch = own.shape[1]
    deep = own.shape[0] - ch
    pre = mm(taps[0], own[:deep]) + mm(taps[1], other[:deep])
    pre_ref[...] = pre
    gated = gelu_tanh(pre).astype(BF)
    hid_own[...] = (ins[0].astype(F32) + mm(gated, own[deep:])).astype(BF)
    hid_other[...] = (ins[1].astype(F32) + mm(gated, other[deep:])).astype(BF)


def owned_kernel(yh_ref, source, out):
    yh = yh_ref[0]
    pos = source.shape[2]
    half = pos // 2
    pairs = source.shape[0] // 4
    left = lax.broadcasted_iota(jnp.int32, source.shape[1:], 1) < half
    for c in range(2):
        for k in range(pairs):
            even = source[4 * k + c].astype(F32)
            odd = source[4 * k + 2 + c].astype(F32)
            first = jnp.where(left, even, pltpu.roll(odd, half, 1))
            second = jnp.where(left, pltpu.roll(even, half, 1), odd)
            at = (c * pairs + k) * pos
            out[:, at : at + pos] = jnp.where(yh == 0, first, second).astype(BF)


def kernel_grad_kernel(owned, everyone, out, total, spaced):
    total[...] = mm(owned[...], everyone[...])
    spaced[...] = jnp.zeros_like(spaced)
    count = spaced.shape[0]
    part = total.shape[0] // count
    for z in range(count):
        spaced[z, :part, :] = total[z * part : (z + 1) * part, :]
    copies = out.shape[0] // count
    for z in range(count):
        for k in range(copies):
            out[z * copies + k] = spaced[z].astype(BF)


def input_grad_kernel(place, by_chip, hidden, own, other, out, grads, spread_, hid, total):
    core, x, yl = place[0], place[1], place[2]
    half, width = out.shape
    pos = 2 * half
    ch = own.shape[1]
    deep = own.shape[0] - ch
    last = by_chip.shape[0] // 2 - 1
    nil = jnp.zeros((half, ch), BF)
    following = by_chip[jnp.minimum(x + 1, last) * 2 + yl]
    before = by_chip[jnp.maximum(x - 1, 0) * 2 + yl]
    grads[:half] = jnp.where(x < last, following, nil)
    grads[half:pos] = nil
    grads[pos : pos + half] = by_chip[x * 2 + yl]
    grads[pos + half : 2 * pos] = nil
    grads[2 * pos : 2 * pos + half] = jnp.where(x > 0, before, nil)
    grads[2 * pos + half :] = nil
    spread_[core] = mm_t(own[:deep], grads[...])
    spread_[1 - core] = mm_t(other[:deep], grads[...])
    flipped = jnp.transpose(jnp.concatenate([hidden[...], jnp.zeros((half, width), F32)]))
    hid[core] = flipped[:ch]
    hid[1 - core] = flipped[ch:]
    granule, count = 24, 16
    for k in range(width // granule):
        block = hid[k % 2, (k // 2) * granule : (k // 2 + 1) * granule, :]
        for tap in range(3):
            row = tap * width + k * granule
            z, c, y = row // 144, (row % 144) // 72, (row % 72) // granule
            at = (y * count + z) * granule
            block = block + spread_[c, at : at + granule, tap * pos : (tap + 1) * pos]
        total[k * granule : (k + 1) * granule, :] = block
    out[...] = jnp.transpose(total[...])[:half]


def rows_of(first, second):
    pos = first.shape[0]
    lane = lax.broadcasted_iota(jnp.int32, (pos, pos), 1)
    return jnp.transpose(jnp.where(lane == 0, first, second))[:2]


def teacher_kernel(member, teacher, member_bias, assay, assay_temp, exp_ref, stats_ref):
    bias = member_bias[pl.ds(member[0], 1), :]
    temps = jnp.zeros(assay.shape, F32)
    for k in range(assay_temp.shape[1]):
        temps = jnp.where(assay[...] == k, assay_temp[:, k : k + 1], temps)
    target = (teacher[...].astype(F32) + bias) / temps
    peak = jnp.max(target, axis=1, keepdims=True)
    exps = jnp.exp(target - peak)
    exp_ref[...] = exps
    stats_ref[...] = rows_of(peak, jnp.sum(exps, axis=1, keepdims=True))


def columns_of(rows, count):
    return jnp.transpose(jnp.concatenate([rows, jnp.zeros((count - rows.shape[0], count), F32)]))


def head_kernel(hid_own, hid_other, own, other, target_stats, exp_ref, stats_ref):
    pos, tracks = exp_ref.shape
    wide = own.shape[2]
    for start in range(0, tracks, wide):
        n = min(wide, tracks - start)
        b = start // wide
        exp_ref[:, start : start + n] = mm(hid_own[...], own[b, :, :n]) + mm(
            hid_other[...], other[b, :, :n]
        )
    peak = jnp.max(exp_ref[...], axis=1, keepdims=True)
    exps = jnp.exp(exp_ref[...] - peak)
    exp_ref[...] = exps
    total = jnp.sum(exps, axis=1, keepdims=True)
    stats_ref[...] = jnp.concatenate([rows_of(peak, total), target_stats[...], jnp.zeros((4, pos), F32)])


def head_back_kernel(yh_ref, exp_s, exp_t, stats, own, other, kept_ref, sent_ref, hg):
    yh = yh_ref[0]
    pos, tracks = exp_s.shape
    wide, ch = own.shape[2], own.shape[1]
    half = pos // 2
    first, second = stats[0], stats[1]
    mine = jnp.where(yh == 0, first, second)

    def scale_of(at):
        top = jnp.maximum(first[at : at + 1], second[at : at + 1])
        total = first[at + 1 : at + 2] * jnp.exp(first[at : at + 1] - top) + second[
            at + 1 : at + 2
        ] * jnp.exp(second[at : at + 1] - top)
        return 2.0 * tracks * jnp.exp(mine[at : at + 1] - top) / total

    scales = columns_of(
        jnp.concatenate([scale_of(0), scale_of(2), jnp.zeros((6, pos), F32)]), pos
    )
    scale_s, scale_t = scales[:, 0:1], scales[:, 1:2]
    grad = (exp_s[...] * scale_s - exp_t[...] * scale_t).astype(BF)
    for source, at in ((own, 0), (other, ch)):
        total = None
        for start in range(0, tracks, wide):
            n = min(wide, tracks - start)
            term = mm_t(grad[:, start : start + n], source[start // wide, :, :n])
            total = term if total is None else total + term
        hg[:, at : at + ch] = total
    kept_ref[...] = hg[pl.ds(pl.multiple_of(yh * half, half), half), :]
    sent_ref[...] = hg[pl.ds(pl.multiple_of((1 - yh) * half, half), half), :].astype(BF)


def back_kernel(yh_ref, kept, received, pre_ref, own, other, grad_ref, hidden_ref):
    yh = yh_ref[0]
    half = kept.shape[0]
    ch = own.shape[1]
    hidden = kept[...] + received[...].astype(F32)
    hidden_ref[...] = hidden
    rounded = hidden.astype(BF)
    deep = own.shape[0] - ch
    gated_grad = mm_t(rounded[:, :ch], own[deep:]) + mm_t(rounded[:, ch:], other[deep:])
    pre = pre_ref[pl.ds(pl.multiple_of(yh * half, half), half), :]
    pre_grad = (gated_grad * gelu_slope(pre)).astype(BF)
    for k in range(grad_ref.shape[0]):
        grad_ref[k] = pre_grad


def on_device(
    inputs, teacher, member, member_bias, assay, assay_temp, conv_weight, proj_weight, head_weight
):
    rows = inputs[0]
    pos, width = rows.shape
    half = pos // 2
    cut, ch = conv_weight.shape
    tracks = head_weight.shape[1]
    zc, cc = lax.axis_size("z"), lax.axis_size(CTX)
    x, yl, core, yh = (lax.axis_index(name) for name in ("x", "yl", "c", "yh"))
    yh_arr = yh.astype(jnp.int32).reshape(1)

    slab = 24
    deep = cut // 2
    deep = cut // 2
    place = jnp.stack([core, yl * 2 + yh, x]).astype(jnp.int32)
    (packed,) = call(
        pack_kernel,
        [SDS((2, slab, ch), BF)],
        [
            pltpu.VMEM(conv_weight.shape, BF),
            pltpu.VMEM(proj_weight.shape, BF),
            pltpu.VMEM(head_weight.shape, BF),
            pltpu.VMEM((cut, ch), F32),
            pltpu.VMEM((2 * slab, 4 * ch), F32),
            pltpu.SemaphoreType.DMA((3,)),
        ],
        2 * slab * width * ch,
        512 * 1024,
        place,
        conv_weight,
        proj_weight,
        head_weight,
        far=(0, 1, 2),
        limit=56,
    )
    gathered = lax.all_gather(packed, "z", axis=0)
    (conv_copies,) = call(
        copies_kernel, [SDS((4, zc, slab, ch), BF)], [], 1024, 1536 * 1024, None, gathered
    )
    over_y = lax.all_to_all(conv_copies, YR, 0, 0).reshape(4 * zc * slab, ch)
    rows_before = shifted(rows, 1)
    rows_after = shifted(rows, -1)
    exp_t, target_stats = call(
        teacher_kernel,
        [SDS((pos, tracks), F32), SDS((2, pos), F32)],
        [],
        4 * pos * tracks,
        1536 * 1024,
        member.astype(jnp.int32),
        teacher[0],
        member_bias,
        assay.reshape(1, tracks),
        assay_temp.reshape(1, assay_temp.shape[0]),
        limit=56,
    )
    own = over_y
    other = swapped(own, "c")

    part = cut // cc
    core_arr = core.astype(jnp.int32).reshape(1)
    taps, kinds, by_owner, head_copies = call(
        prepare_kernel,
        [
            SDS((2, pos, zc * deep), BF),
            SDS((2, pos, ch), BF),
            SDS((cc, zc * part, pos), BF),
            SDS((4, zc, slab, ch), BF),
        ],
        [
            pltpu.VMEM((3 * width, pos), F32),
            pltpu.VMEM((2, zc * deep, pos), F32),
            pltpu.VMEM((2, ch, pos), F32),
            pltpu.VMEM((cc, zc * part, pos), F32),
            pltpu.VMEM((2, pos, zc * deep), BF),
            pltpu.VMEM((2, pos, ch), BF),
            pltpu.VMEM((cc, zc * part, pos), BF),
            pltpu.SemaphoreType.DMA((7,)),
        ],
        2 * pos * pos * 3 * width,
        2 * 1024 * 1024,
        core_arr,
        rows_before,
        rows,
        rows_after,
        gathered,
        target_stats,
        far_out=(0, 1, 2, 3),
        limit=56,
    )
    head_own = lax.all_to_all(head_copies, "x", 0, 0).reshape(4, zc * slab, ch)
    pre_act, hid_own, hid_other = call(
        conv_kernel,
        [SDS((pos, ch), F32), SDS((pos, ch), BF), SDS((pos, ch), BF)],
        [],
        2 * pos * ch * 4 * width,
        3 * 1024 * 1024,
        None,
        taps,
        kinds,
        own,
        other,
    )

    head_other = swapped(head_own, "c")

    owned = lax.all_to_all(by_owner, CTX, 0, 0)
    (owned,) = call(
        owned_kernel,
        [SDS((zc * part, cc * half), BF)],
        [],
        1024 * 1024,
        1024 * 1024,
        yh_arr,
        owned,
    )

    exp_s, stats = call(
        head_kernel,
        [SDS((pos, tracks), F32), SDS((8, pos), F32)],
        [],
        2 * pos * width * tracks,
        4 * 1024 * 1024,
        None,
        hid_own,
        hid_other,
        head_own,
        head_other,
        target_stats,
    )
    stats = lax.all_gather(stats, "yh", axis=0)
    kept, sent = call(
        head_back_kernel,
        [SDS((half, width), F32), SDS((half, width), BF)],
        [pltpu.VMEM((pos, width), F32)],
        2 * pos * width * tracks,
        4 * 1024 * 1024,
        yh_arr,
        exp_s,
        exp_t,
        stats,
        head_own,
        head_other,
    )
    received = swapped(sent, "yh")
    copies, hidden_grad = call(
        back_kernel,
        [SDS((cc // 2, half, ch), BF), SDS((half, width), F32)],
        [],
        2 * half * width * ch,
        2 * 1024 * 1024,
        yh_arr,
        kept,
        received,
        pre_act,
        own,
        other,
    )

    by_chip = lax.all_to_all(copies, ("x", "yl"), 0, 0)
    everyone = lax.all_gather(by_chip.reshape(cc // 2 * half, ch), "c", axis=0, tiled=True)
    padded = 16
    (kernel_part,) = call(
        kernel_grad_kernel,
        [SDS((zc, padded, ch), BF)],
        [pltpu.VMEM((zc * part, ch), F32), pltpu.VMEM((zc, padded, ch), F32)],
        2 * zc * part * cc * half * ch,
        2 * 1024 * 1024,
        None,
        owned,
        everyone,
    )
    terms = lax.all_to_all(kernel_part, "z", 0, 0)
    kernel_sum = jnp.sum(terms.astype(F32), axis=0)[:part]
    kernel_pair = lax.all_gather(kernel_sum, "yh", axis=0)
    grad_conv = (kernel_pair[0] + kernel_pair[1]) / math.sqrt(zc * cc * pos)

    (grad_rows,) = call(
        input_grad_kernel,
        [SDS((half, width), F32)],
        [
            pltpu.VMEM((3 * pos, ch), BF),
            pltpu.VMEM((2, zc * deep, 3 * pos), F32),
            pltpu.VMEM((2, ch, pos), F32),
            pltpu.VMEM((width, pos), F32),
        ],
        4 * half * width * ch,
        2 * 1024 * 1024,
        jnp.stack([core, x, yl]).astype(jnp.int32),
        by_chip,
        hidden_grad,
        own,
        other,
    )
    grad_other = swapped(grad_rows, "yh")
    grad_input = jnp.where(
        yh == 0,
        jnp.concatenate([grad_rows, grad_other], axis=0),
        jnp.concatenate([grad_other, grad_rows], axis=0),
    )
    return (grad_input[None], grad_conv)


def solution(mesh):
    fine = Mesh(mesh.devices.reshape(16, 4, 2, 2, 2), ("z", "x", "yl", "c", "yh"))
    return jax.shard_map(
        on_device,
        mesh=fine,
        in_specs=(
            P("z", CTX, None),
            P("z", CTX, "yh"),
            P("z"),
            P(None, "yh"),
            P("yh"),
            P(),
            P("z", None),
            P("z", None),
            P("z", "yh"),
        ),
        out_specs=(P("z", CTX, None), P(("z",) + CTX, None)),
        check_vma=False,
    )
```

time: 195 us -> 154 us (0.79)
  the two profiles are of different devices: /device:TPU:16 before, /device:TPU:56 now
where the time goes in v2:
time: 154 us; the launch traced here: 153 us
  blocking collectives  50.8 us (33%)
  starting transfers between devices  45 us (29%)
  waiting for transfers between devices  30.9 us (20%)
  Pallas kernels  19.6 us (13%)
  local copies, waits for them, and re-layouts  3.33 us (2%)
  other arithmetic  2.16 us (1%)
    all_gather x1, blocking collectives, on_device(): gathered = lax.all_gather(packed, 'z', axis=0)  36.6 us
    pallas_call x11, Pallas kernels, call(): pl.pallas_call(body, out_shape=outs, in_specs=specs, out_specs=[spec(k, f...  19.6 us
    ppermute x4, waiting for transfers between devices, swapped(): return lax.ppermute(value, axis, [(0, 1), (1, 0)])  12.1 us
    all_to_all x1, waiting for transfers between devices, on_device(): head_own = lax.all_to_all(head_copies, 'x', 0, 0).reshape(4, zc * slab, ch)  9.68 us
    ppermute x4, starting transfers between devices, swapped(): return lax.ppermute(value, axis, [(0, 1), (1, 0)])  9.55 us
    all_to_all x1, starting transfers between devices, on_device(): terms = lax.all_to_all(kernel_part, 'z', 0, 0)  9.14 us
    all_gather x1, blocking collectives, on_device(): kernel_pair = lax.all_gather(kernel_sum, 'yh', axis=0)  6.01 us
    all_gather x1, blocking collectives, on_device(): stats = lax.all_gather(stats, 'yh', axis=0)  5.85 us
  transfers between devices with their start and end apart: 11, of which 5 were waited for; matrix products, arithmetic and copies ran while one was open for 1% of the time, Pallas kernels for 10%

profile of v2, /device:TPU:56, one launch (start us, length us, event | category | flops | bytes accessed | tf_op | source)
XLA Modules:
  0.0 153.3 jit_solution(6700462022667470559)
XLA Ops:
  1.3 2.3 %shard_map.104 = bf16[2,24,384]{2,1,0:T(8,128)(2,1)} custom-call(s32[3]{0:T(128)} %pad_add_fusion.1.place, bf16[144,384]{1,0:T(8,128)(2,1)} %conv_far.1, bf16[24,768]{1,0:T(8,128)(2,1)} %proj_far.1, bf16[48,1408]{1,0:T(8,128)(2,1)} %head_far.1), custom_call_target="tpu_custom_call" | custom-call | flops 14155776 | bytes 524288 | tf_op jit(solution)/shard_map/pallas_call | solution.py:61
  3.6 36.6 %all-gather = bf16[32,24,384]{2,1,0:T(8,128)(2,1)S(1)} all-gather(bf16[2,24,384]{2,1,0:T(8,128)(2,1)} %shard_map.104), channel_id=2, replica_groups=mesh['z'=16,'x'=4,'yl'=2,'c'=2,'yh'=2] {'z'}, dimensions={0}, use_global_device_ids=true | all-gather | bytes 626688 | tf_op jit(solution)/shard_map/all_gather | solution.py:345
  41.5 4.8 %all-to-all-start = ((bf16[4,16,24,384]{3,2,1,0:T(8,128)(2,1)}), bf16[4,16,24,384]{3,2,1,0:T(8,128)(2,1)S(1)}, u32[]{:S(2)}, u32[]{:S(2)}) async-start(bf16[4,16,24,384]{3,2,1,0:T(8,128)(2,1)} %shard_map.107), calls=%async_computation | async-start | bytes 2359296 | tf_op jit(solution)/shard_map/all_to_all | solution.py:349
  47.6 4.6 %collective-permute-start = (bf16[128,768]{1,0:T(8,128)(2,1)S(1)}, bf16[128,768]{1,0:T(8,128)(2,1)S(1)}, u32[]{:S(2)}, u32[]{:S(2)}) collective-permute-start(bf16[128,768]{1,0:T(8,128)(2,1)S(1)} %bitcast.34), channel_id=1, source_target_pairs={{0,8},{8,16},{16,24},{1,9},{9,17},{17,25},{2,10},{10,18},{18,26},{... | collective-permute-start | bytes 589832 | tf_op jit(solution)/shard_map/ppermute | solution.py:46
  53.4 2.1 %shard_map.105 = (f32[128,1408]{1,0:T(8,128)}, f32[2,128]{1,0:T(2,128)}) custom-call(s32[1]{0:T(128)S(6)} %copy.11.member, bf16[128,1408]{1,0:T(8,128)(2,1)} %bitcast.31, f32[4,1408]{1,0:T(4,128)} %member_bias.1, s32[1,1408]{1,0:T(1,128)} %reshape.82.assay, f32[1,4]{1,0:T(1,128)} %bitcast.36), custom_call_target="tpu_custom_call" | custom-call | flops 720896 | bytes 1572864 | tf_op jit(solution)/shard_map/pallas_call | solution.py:61
  56.3 3.3 %shard_map.106 = (bf16[2,128,1152]{2,1,0:T(8,128)(2,1)}, bf16[2,128,384]{2,1,0:T(8,128)(2,1)}, bf16[16,144,128]{2,1,0:T(8,128)(2,1)}, bf16[4,16,24,384]{3,2,1,0:T(8,128)(2,1)}) custom-call(s32[1]{0:T(128)} %bitcast.core_ref, bf16[128,768]{1,0:T(8,128)(2,1)} %copy-done.7, bf16[128,768]{1,0:T(8,128)(2,1)} %bitcast.32, bf16[128,768]{1,0:T(8,128)(2,1)} %copy-done.6, ...), custom_call_target="tpu_custom_call" | custom-call | flops 75497472 | bytes 2097152 | tf_op jit(solution)/shard_map/pallas_call | solution.py:61
  59.6 5.0 %all-to-all-start.1 = ((bf16[4,16,24,384]{3,2,1,0:T(8,128)(2,1)}), bf16[4,16,24,384]{3,2,1,0:T(8,128)(2,1)S(1)}, u32[]{:S(2)}, u32[]{:S(2)}) async-start(bf16[4,16,24,384]{3,2,1,0:T(8,128)(2,1)} %get-tuple-element.22), calls=%async_computation.1 | async-start | bytes 2359296 | tf_op jit(solution)/shard_map/all_to_all | solution.py:399
  66.6 9.7 %all-to-all-done.1 = bf16[4,16,24,384]{3,2,1,0:T(8,128)(2,1)S(1)} async-done(((bf16[4,16,24,384]{3,2,1,0:T(8,128)(2,1)}), bf16[4,16,24,384]{3,2,1,0:T(8,128)(2,1)S(1)}, u32[]{:S(2)}, u32[]{:S(2)}) %all-to-all-start.1) | async-done | bytes 1179680 | tf_op jit(solution)/shard_map/all_to_all | solution.py:399
  76.2 1.9 %collective-permute-start.3 = (bf16[4,384,384]{2,1,0:T(8,128)(2,1)S(1)}, bf16[4,384,384]{2,1,0:T(8,128)(2,1)}, u32[]{:S(2)}, u32[]{:S(2)}) collective-permute-start(bf16[4,384,384]{2,1,0:T(8,128)(2,1)S(1)} %bitcast.23), channel_id=1, source_target_pairs={{0,2},{2,0},{1,3},{3,1},{4,6},{6,4},{5,7},{7,5},{8,10},{10,8},{9,1... | collective-permute-start | bytes 3538952 | tf_op jit(solution)/shard_map/ppermute | solution.py:50
  78.2 4.9 %all-to-all-start.3 = ((bf16[16,144,128]{2,1,0:T(8,128)(2,1)}), bf16[16,144,128]{2,1,0:T(8,128)(2,1)}, u32[]{:S(2)}, u32[]{:S(2)}) async-start(bf16[16,144,128]{2,1,0:T(8,128)(2,1)} %get-tuple-element.31), calls=%async_computation.3 | async-start | bytes 1179648 | tf_op jit(solution)/shard_map/all_to_all | solution.py:415
  85.8 2.2 %shard_map.109 = (f32[128,1408]{1,0:T(8,128)S(1)}, f32[8,128]{1,0:T(8,128)S(1)}) custom-call(bf16[128,384]{1,0:T(8,128)(2,1)S(1)} %get-tuple-element.20.hid_own, bf16[128,384]{1,0:T(8,128)(2,1)S(1)} %get-tuple-element.21.hid_other, bf16[4,384,384]{2,1,0:T(8,128)(2,1)S(1)} %bitcast.24, bf16[4,384,384]{2,1,0:T(8,128)(2,1)} %collective-permute-done.3.other, ...), custom_call_target="tpu_custom_call" | custom-call | flops 276824064 | bytes 4194304 | tf_op jit(solution)/shard_map/pallas_call | solution.py:61
  88.0 5.8 %all-gather.1 = f32[16,128]{1,0:T(8,128)S(1)} all-gather(f32[8,128]{1,0:T(8,128)S(1)} %get-tuple-element.25), channel_id=3, replica_groups=mesh['z'=16,'x'=4,'yl'=2,'c'=2,'yh'=2] {'yh'}, dimensions={0}, use_global_device_ids=true | all-gather | bytes 12288 | tf_op jit(solution)/shard_map/all_gather | solution.py:439
  93.8 2.3 %shard_map.110 = (f32[64,768]{1,0:T(8,128)S(1)}, bf16[64,768]{1,0:T(8,128)(2,1)S(1)}) custom-call(s32[1]{0:T(128)} %bitcast.3.yh_ref, f32[128,1408]{1,0:T(8,128)S(1)} %get-tuple-element.23.exp_s, f32[128,1408]{1,0:T(8,128)S(1)} %copy-done.1, f32[2,8,128]{2,1,0:T(8,128)S(1)} %bitcast.30, bf16[4,384,384]{2,1,0:T(8,128)(2,1)S(1)} %bitcast.25, ...), custom_call_target="tpu_custom_call" | custom-call | flops 276824064 | bytes 4194304 | tf_op jit(solution)/shard_map/pallas_call | solution.py:61
  96.1 3.1 %collective-permute-start.4 = (bf16[64,768]{1,0:T(8,128)(2,1)S(1)}, bf16[64,768]{1,0:T(8,128)(2,1)S(1)}, u32[]{:S(2)}, u32[]{:S(2)}) collective-permute-start(bf16[64,768]{1,0:T(8,128)(2,1)S(1)} %get-tuple-element.27), channel_id=1, source_target_pairs={{0,1},{1,0},{2,3},{3,2},{4,5},{5,4},{6,7},{7,6},{8,9},{9,8},{10,11... | collective-permute-start | bytes 294920 | tf_op jit(solution)/shard_map/ppermute | solution.py:50
  99.2 5.0 %collective-permute-done.4.received = bf16[64,768]{1,0:T(8,128)(2,1)S(1)} collective-permute-done((bf16[64,768]{1,0:T(8,128)(2,1)S(1)}, bf16[64,768]{1,0:T(8,128)(2,1)S(1)}, u32[]{:S(2)}, u32[]{:S(2)}) %collective-permute-start.4) | collective-permute-done | bytes 98336 | tf_op jit(solution)/shard_map/ppermute | solution.py:50
  105.3 5.8 %all-to-all-start.2 = ((bf16[8,64,384]{2,1,0:T(8,128)(2,1)}), bf16[8,64,384]{2,1,0:T(8,128)(2,1)S(1)}, u32[]{:S(2)}, u32[]{:S(2)}) async-start(bf16[8,64,384]{2,1,0:T(8,128)(2,1)} %get-tuple-element.29), calls=%async_computation.2 | async-start | bytes 786432 | tf_op jit(solution)/shard_map/all_to_all | solution.py:468
  112.3 5.5 %all-to-all-done.2.by_chip = bf16[8,64,384]{2,1,0:T(8,128)(2,1)S(1)} async-done(((bf16[8,64,384]{2,1,0:T(8,128)(2,1)}), bf16[8,64,384]{2,1,0:T(8,128)(2,1)S(1)}, u32[]{:S(2)}, u32[]{:S(2)}) %all-to-all-start.2) | async-done | bytes 393248 | tf_op jit(solution)/shard_map/all_to_all | solution.py:468
  117.8 2.4 %all_gather.25.everyone = bf16[1024,384]{1,0:T(8,128)(2,1)S(1)} all-gather(bf16[512,384]{1,0:T(8,128)(2,1)S(1)} %bitcast.28), channel_id=1, replica_groups=mesh['z'=16,'x'=4,'yl'=2,'c'=2,'yh'=2] {'c'}, dimensions={0}, use_global_device_ids=true | all-gather | bytes 1179648 | tf_op jit(solution)/shard_map/all_gather | solution.py:469
  121.2 9.1 %all-to-all-start.4 = ((bf16[16,16,384]{2,1,0:T(8,128)(2,1)}), bf16[16,16,384]{2,1,0:T(8,128)(2,1)S(1)}, u32[]{:S(2)}, u32[]{:S(2)}) async-start(bf16[16,16,384]{2,1,0:T(8,128)(2,1)} %shard_map.114), calls=%async_computation.4 | async-start | bytes 393216 | tf_op jit(solution)/shard_map/all_to_all | solution.py:481
  130.5 1.9 %shard_map.112 = f32[64,768]{1,0:T(8,128)S(1)} custom-call(s32[3]{0:T(128)S(1)} %pad_add_fusion.place, bf16[8,64,384]{2,1,0:T(8,128)(2,1)S(1)} %all-to-all-done.2.by_chip, f32[64,768]{1,0:T(8,128)S(1)} %get-tuple-element.30.hidden, bf16[1536,384]{1,0:T(8,128)(2,1)S(1)} %bitcast.22, bf16[1536,384]{1,0:T(8,128)(2,1)S(1)} %collective-permute-done.2.other), custom_call_target="tpu_custom_call" | custom-call | flops 75497472 | bytes 2097152 | tf_op jit(solution)/shard_map/pallas_call | solution.py:61
  132.4 2.7 %collective-permute-start.5 = (f32[64,768]{1,0:T(8,128)S(1)}, f32[64,768]{1,0:T(8,128)S(1)}, u32[]{:S(2)}, u32[]{:S(2)}) collective-permute-start(f32[64,768]{1,0:T(8,128)S(1)} %shard_map.112), channel_id=1, source_target_pairs={{0,1},{1,0},{2,3},{3,2},{4,5},{5,4},{6,7},{7,6},{8,9},{9,8},{10,11... | collective-permute-start | bytes 589832 | tf_op jit(solution)/shard_map/ppermute | solution.py:50
  135.1 7.1 %collective-permute-done.5 = f32[64,768]{1,0:T(8,128)S(1)} collective-permute-done((f32[64,768]{1,0:T(8,128)S(1)}, f32[64,768]{1,0:T(8,128)S(1)}, u32[]{:S(2)}, u32[]{:S(2)}) %collective-permute-start.5) | collective-permute-done | bytes 196640 | tf_op jit(solution)/shard_map/ppermute | solution.py:50
  143.0 3.6 %all-to-all-done.4 = bf16[16,16,384]{2,1,0:T(8,128)(2,1)S(1)} async-done(((bf16[16,16,384]{2,1,0:T(8,128)(2,1)}), bf16[16,16,384]{2,1,0:T(8,128)(2,1)S(1)}, u32[]{:S(2)}, u32[]{:S(2)}) %all-to-all-start.4) | async-done | bytes 196640 | tf_op jit(solution)/shard_map/all_to_all | solution.py:481
  146.7 6.0 %all-gather.3 = f32[2,9,384]{2,1,0:T(8,128)S(1)} all-gather(f32[1,9,384]{2,1,0:T(8,128)S(1)} %slice_bitcast_fusion), channel_id=4, replica_groups=mesh['z'=16,'x'=4,'yl'=2,'c'=2,'yh'=2] {'yh'}, dimensions={0}, use_global_device_ids=true | all-gather | bytes 41472 | tf_op jit(solution)/shard_map/all_gather | solution.py:483
  (38 shorter events, 14.1 us)
Async XLA Ops:
  40.3 1.2 copy-start
  41.5 4.8 %copy-start.5 = (bf16[1,128,768]{2,1,0:T(8,128)(2,1)S(1)}, bf16[1,128,768]{2,1,0:T(8,128)(2,1)}, u32[]{:S(2)}) copy-start(bf16[1,128,768]{2,1,0:T(8,128)(2,1)} %param.9) | copy-start | bytes 589828
  41.5 11.3 %copy-start.8 = (s32[1408]{0:T(1024)S(1)}, s32[1408]{0:T(1024)}, u32[]{:S(2)}) copy-start(s32[1408]{0:T(1024)} %param.13) | copy-start | bytes 16900
  41.5 18.1 %all-to-all-start = ((bf16[4,16,24,384]{3,2,1,0:T(8,128)(2,1)}), bf16[4,16,24,384]{3,2,1,0:T(8,128)(2,1)S(1)}, u32[]{:S(2)}, u32[]{:S(2)}) async-start(bf16[4,16,24,384]{3,2,1,0:T(8,128)(2,1)} %shard_map.107), calls=%async_computation | async-start | bytes 2359296 | tf_op jit(solution)/shard_map/all_to_all | solution.py:349
  46.3 9.3 %collective-permute-start.1 = (bf16[128,768]{1,0:T(8,128)(2,1)S(1)}, bf16[128,768]{1,0:T(8,128)(2,1)S(1)}, u32[]{:S(2)}, u32[]{:S(2)}) collective-permute-start(bf16[128,768]{1,0:T(8,128)(2,1)S(1)} %bitcast.33), channel_id=1, source_target_pairs={{8,0},{16,8},{24,16},{9,1},{17,9},{25,17},{10,2},{18,10},{26,18},{... | collective-permute-start | bytes 589832 | tf_op jit(solution)/shard_map/ppermute | solution.py:46
  47.6 8.0 %collective-permute-start = (bf16[128,768]{1,0:T(8,128)(2,1)S(1)}, bf16[128,768]{1,0:T(8,128)(2,1)S(1)}, u32[]{:S(2)}, u32[]{:S(2)}) collective-permute-start(bf16[128,768]{1,0:T(8,128)(2,1)S(1)} %bitcast.34), channel_id=1, source_target_pairs={{0,8},{8,16},{16,24},{1,9},{9,17},{17,25},{2,10},{10,18},{18,26},{... | collective-permute-start | bytes 589832 | tf_op jit(solution)/shard_map/ppermute | solution.py:46
  55.6 0.7 copy-start.6
  55.6 0.7 copy-start.7
  59.6 16.6 %all-to-all-start.1 = ((bf16[4,16,24,384]{3,2,1,0:T(8,128)(2,1)}), bf16[4,16,24,384]{3,2,1,0:T(8,128)(2,1)S(1)}, u32[]{:S(2)}, u32[]{:S(2)}) async-start(bf16[4,16,24,384]{3,2,1,0:T(8,128)(2,1)} %get-tuple-element.22), calls=%async_computation.1 | async-start | bytes 2359296 | tf_op jit(solution)/shard_map/all_to_all | solution.py:399
  64.6 18.4 %collective-permute-start.2 = (bf16[1536,384]{1,0:T(8,128)(2,1)S(1)}, bf16[1536,384]{1,0:T(8,128)(2,1)S(1)}, u32[]{:S(2)}, u32[]{:S(2)}) collective-permute-start(bf16[1536,384]{1,0:T(8,128)(2,1)S(1)} %bitcast.19), channel_id=1, source_target_pairs={{0,2},{2,0},{1,3},{3,1},{4,6},{6,4},{5,7},{7,5},{8,10},{10,8},{9,1... | collective-permute-start | bytes 3538952 | tf_op jit(solution)/shard_map/ppermute | solution.py:50
  76.2 9.5 %collective-permute-start.3 = (bf16[4,384,384]{2,1,0:T(8,128)(2,1)S(1)}, bf16[4,384,384]{2,1,0:T(8,128)(2,1)}, u32[]{:S(2)}, u32[]{:S(2)}) collective-permute-start(bf16[4,384,384]{2,1,0:T(8,128)(2,1)S(1)} %bitcast.23), channel_id=1, source_target_pairs={{0,2},{2,0},{1,3},{3,1},{4,6},{6,4},{5,7},{7,5},{8,10},{10,8},{9,1... | collective-permute-start | bytes 3538952 | tf_op jit(solution)/shard_map/ppermute | solution.py:50
  78.2 27.1 %all-to-all-start.3 = ((bf16[16,144,128]{2,1,0:T(8,128)(2,1)}), bf16[16,144,128]{2,1,0:T(8,128)(2,1)}, u32[]{:S(2)}, u32[]{:S(2)}) async-start(bf16[16,144,128]{2,1,0:T(8,128)(2,1)} %get-tuple-element.31), calls=%async_computation.3 | async-start | bytes 1179648 | tf_op jit(solution)/shard_map/all_to_all | solution.py:415
  83.0 1.1 copy-start.2
  84.1 0.9 copy-start.3
  85.0 0.8 copy-start.4
  85.8 8.1 %copy-start.1 = (f32[128,1408]{1,0:T(8,128)S(1)}, f32[128,1408]{1,0:T(8,128)}, u32[]{:S(2)}) copy-start(f32[128,1408]{1,0:T(8,128)} %get-tuple-element.24.exp_t) | copy-start | bytes 2162692
  96.1 8.0 %collective-permute-start.4 = (bf16[64,768]{1,0:T(8,128)(2,1)S(1)}, bf16[64,768]{1,0:T(8,128)(2,1)S(1)}, u32[]{:S(2)}, u32[]{:S(2)}) collective-permute-start(bf16[64,768]{1,0:T(8,128)(2,1)S(1)} %get-tuple-element.27), channel_id=1, source_target_pairs={{0,1},{1,0},{2,3},{3,2},{4,5},{5,4},{6,7},{7,6},{8,9},{9,8},{10,11... | collective-permute-start | bytes 294920 | tf_op jit(solution)/shard_map/ppermute | solution.py:50
  105.3 12.6 %all-to-all-start.2 = ((bf16[8,64,384]{2,1,0:T(8,128)(2,1)}), bf16[8,64,384]{2,1,0:T(8,128)(2,1)S(1)}, u32[]{:S(2)}, u32[]{:S(2)}) async-start(bf16[8,64,384]{2,1,0:T(8,128)(2,1)} %get-tuple-element.29), calls=%async_computation.2 | async-start | bytes 786432 | tf_op jit(solution)/shard_map/all_to_all | solution.py:468
  121.2 25.4 %all-to-all-start.4 = ((bf16[16,16,384]{2,1,0:T(8,128)(2,1)}), bf16[16,16,384]{2,1,0:T(8,128)(2,1)S(1)}, u32[]{:S(2)}, u32[]{:S(2)}) async-start(bf16[16,16,384]{2,1,0:T(8,128)(2,1)} %shard_map.114), calls=%async_computation.4 | async-start | bytes 393216 | tf_op jit(solution)/shard_map/all_to_all | solution.py:481
  132.4 9.8 %collective-permute-start.5 = (f32[64,768]{1,0:T(8,128)S(1)}, f32[64,768]{1,0:T(8,128)S(1)}, u32[]{:S(2)}, u32[]{:S(2)}) collective-permute-start(f32[64,768]{1,0:T(8,128)S(1)} %shard_map.112), channel_id=1, source_target_pairs={{0,1},{1,0},{2,3},{3,2},{4,5},{5,4},{6,7},{7,6},{8,9},{9,8},{10,11... | collective-permute-start | bytes 589832 | tf_op jit(solution)/shard_map/ppermute | solution.py:50

commit v3 on v2

--- a/solution.py
+++ b/solution.py
@@ -69,8 +69,9 @@
     )(*args)
 
 
-def pack_kernel(place, conv_far, proj_far, head_far, out, conv, proj, head, conv_wide, head_wide, sems):
-    core, y, x = place[0], place[1], place[2]
+def pack_kernel(conv_far, proj_far, head_far, out, conv, proj, head, conv_wide, head_wide, sems):
+    core, x = lax.axis_index("c"), lax.axis_index("x")
+    y = lax.axis_index("yl") * 2 + lax.axis_index("yh")
     loads = [
         pltpu.make_async_copy(far, near, sems.at[k])
         for k, (far, near) in enumerate(((proj_far, proj), (conv_far, conv), (head_far, head)))
@@ -148,16 +149,17 @@
         store.wait()
 
 
-def conv_kernel(
-    taps, ins, own, other, pre_ref, hid_own, hid_other
-):
-    ch = own.shape[1]
-    deep = own.shape[0] - ch
+def conv_kernel(taps, own, other, pre_ref, gated_ref):
+    deep = taps.shape[2]
     pre = mm(taps[0], own[:deep]) + mm(taps[1], other[:deep])
     pre_ref[...] = pre
-    gated = gelu_tanh(pre).astype(BF)
-    hid_own[...] = (ins[0].astype(F32) + mm(gated, own[deep:])).astype(BF)
-    hid_other[...] = (ins[1].astype(F32) + mm(gated, other[deep:])).astype(BF)
+    gated_ref[...] = gelu_tanh(pre).astype(BF)
+
+
+def hidden_kernel(gated, ins, own, other, hid_own, hid_other):
+    deep = own.shape[0] - own.shape[1]
+    hid_own[...] = (ins[0].astype(F32) + mm(gated[...], own[deep:])).astype(BF)
+    hid_other[...] = (ins[1].astype(F32) + mm(gated[...], other[deep:])).astype(BF)
 
 
 def owned_kernel(yh_ref, source, out):
@@ -230,9 +232,10 @@
 
 def teacher_kernel(member, teacher, member_bias, assay, assay_temp, exp_ref, stats_ref):
     bias = member_bias[pl.ds(member[0], 1), :]
-    temps = jnp.zeros(assay.shape, F32)
+    groups = assay[...][None, :]
+    temps = jnp.zeros(groups.shape, F32)
     for k in range(assay_temp.shape[1]):
-        temps = jnp.where(assay[...] == k, assay_temp[:, k : k + 1], temps)
+        temps = jnp.where(groups == k, assay_temp[:, k : k + 1], temps)
     target = (teacher[...].astype(F32) + bias) / temps
     peak = jnp.max(target, axis=1, keepdims=True)
     exps = jnp.exp(target - peak)
@@ -321,7 +324,6 @@
     slab = 24
     deep = cut // 2
     deep = cut // 2
-    place = jnp.stack([core, yl * 2 + yh, x]).astype(jnp.int32)
     (packed,) = call(
         pack_kernel,
         [SDS((2, slab, ch), BF)],
@@ -335,7 +337,7 @@
         ],
         2 * slab * width * ch,
         512 * 1024,
-        place,
+        None,
         conv_weight,
         proj_weight,
         head_weight,
@@ -358,7 +360,7 @@
         member.astype(jnp.int32),
         teacher[0],
         member_bias,
-        assay.reshape(1, tracks),
+        assay,
         assay_temp.reshape(1, assay_temp.shape[0]),
         limit=56,
     )
@@ -397,19 +399,29 @@
         limit=56,
     )
     head_own = lax.all_to_all(head_copies, "x", 0, 0).reshape(4, zc * slab, ch)
-    pre_act, hid_own, hid_other = call(
+    pre_act, gated = call(
         conv_kernel,
-        [SDS((pos, ch), F32), SDS((pos, ch), BF), SDS((pos, ch), BF)],
+        [SDS((pos, ch), F32), SDS((pos, ch), BF)],
         [],
-        2 * pos * ch * 4 * width,
+        2 * pos * ch * 3 * width,
         3 * 1024 * 1024,
         None,
         taps,
+        own,
+        other,
+    )
+    hid_own, hid_other = call(
+        hidden_kernel,
+        [SDS((pos, ch), BF), SDS((pos, ch), BF)],
+        [],
+        2 * pos * ch * width,
+        1024 * 1024,
+        None,
+        gated,
         kinds,
         own,
         other,
     )
-
     head_other = swapped(head_own, "c")
 
     owned = lax.all_to_all(by_owner, CTX, 0, 0)

time: 154 us -> 153 us (level)
    pallas_call x11 -> x12, Pallas kernels: 19.6 us -> 19 us  [call(): pl.pallas_call(body, out_shape=outs, in_specs=specs, out_specs=[spec(k, f...]
  transfers between devices with their start and end apart: 11 -> 11, of which waited for: 5 -> 6; matrix products, arithmetic and copies ran while one was open for 1% -> 1% of each run, Pallas kernels for 10% -> 10%
where the time goes in v3:
time: 153 us; the launch traced here: 152 us
  blocking collectives  50.8 us (33%)
  starting transfers between devices  45.4 us (30%)
  waiting for transfers between devices  31.1 us (20%)
  Pallas kernels  19 us (12%)
  local copies, waits for them, and re-layouts  2.53 us (2%)
    all_gather x1, blocking collectives, on_device(): gathered = lax.all_gather(packed, 'z', axis=0)  36.6 us
    pallas_call x12, Pallas kernels, call(): pl.pallas_call(body, out_shape=outs, in_specs=specs, out_specs=[spec(k, f...  19 us
    ppermute x4, waiting for transfers between devices, swapped(): return lax.ppermute(value, axis, [(0, 1), (1, 0)])  11.9 us
    all_to_all x1, waiting for transfers between devices, on_device(): head_own = lax.all_to_all(head_copies, 'x', 0, 0).reshape(4, zc * slab, ch)  9.68 us
    ppermute x4, starting transfers between devices, swapped(): return lax.ppermute(value, axis, [(0, 1), (1, 0)])  9.66 us
    all_to_all x1, starting transfers between devices, on_device(): terms = lax.all_to_all(kernel_part, 'z', 0, 0)  9.15 us
    all_gather x1, blocking collectives, on_device(): kernel_pair = lax.all_gather(kernel_sum, 'yh', axis=0)  6.01 us
    all_gather x1, blocking collectives, on_device(): stats = lax.all_gather(stats, 'yh', axis=0)  5.85 us
  transfers between devices with their start and end apart: 11, of which 6 were waited for; matrix products, arithmetic and copies ran while one was open for 1% of the time, Pallas kernels for 10%

profile of v3, /device:TPU:56, one launch (start us, length us, event | category | flops | bytes accessed | tf_op | source)
XLA Modules:
  0.0 151.8 jit_solution(1192652692401867394)
XLA Ops:
  2.3 36.6 %all-gather = bf16[32,24,384]{2,1,0:T(8,128)(2,1)S(1)} all-gather(bf16[2,24,384]{2,1,0:T(8,128)(2,1)} %shard_map.104), channel_id=2, replica_groups=mesh['z'=16,'x'=4,'yl'=2,'c'=2,'yh'=2] {'z'}, dimensions={0}, use_global_device_ids=true | all-gather | bytes 626688 | tf_op jit(solution)/shard_map/all_gather | solution.py:347
  40.2 4.8 %all-to-all-start = ((bf16[4,16,24,384]{3,2,1,0:T(8,128)(2,1)}), bf16[4,16,24,384]{3,2,1,0:T(8,128)(2,1)S(1)}, u32[]{:S(2)}, u32[]{:S(2)}) async-start(bf16[4,16,24,384]{3,2,1,0:T(8,128)(2,1)} %shard_map.107), calls=%async_computation | async-start | bytes 2359296 | tf_op jit(solution)/shard_map/all_to_all | solution.py:351
  46.3 4.6 %collective-permute-start = (bf16[128,768]{1,0:T(8,128)(2,1)S(1)}, bf16[128,768]{1,0:T(8,128)(2,1)S(1)}, u32[]{:S(2)}, u32[]{:S(2)}) collective-permute-start(bf16[128,768]{1,0:T(8,128)(2,1)S(1)} %bitcast.34), channel_id=1, source_target_pairs={{0,8},{8,16},{16,24},{1,9},{9,17},{17,25},{2,10},{10,18},{18,26},{... | collective-permute-start | bytes 589832 | tf_op jit(solution)/shard_map/ppermute | solution.py:46
  51.5 2.2 %shard_map.105 = (f32[128,1408]{1,0:T(8,128)}, f32[2,128]{1,0:T(2,128)}) custom-call(s32[1]{0:T(128)S(6)} %copy.11.member, bf16[128,1408]{1,0:T(8,128)(2,1)} %bitcast.31, f32[4,1408]{1,0:T(4,128)} %member_bias.1, s32[1408]{0:T(1024)} %assay.1, f32[1,4]{1,0:T(1,128)} %bitcast.36), custom_call_target="tpu_custom_call" | custom-call | flops 720896 | bytes 1572864 | tf_op jit(solution)/shard_map/pallas_call | solution.py:61
  54.7 3.3 %shard_map.106 = (bf16[2,128,1152]{2,1,0:T(8,128)(2,1)}, bf16[2,128,384]{2,1,0:T(8,128)(2,1)}, bf16[16,144,128]{2,1,0:T(8,128)(2,1)}, bf16[4,16,24,384]{3,2,1,0:T(8,128)(2,1)}) custom-call(s32[1]{0:T(128)} %bitcast.core_ref, bf16[128,768]{1,0:T(8,128)(2,1)} %copy-done.7, bf16[128,768]{1,0:T(8,128)(2,1)} %bitcast.32, bf16[128,768]{1,0:T(8,128)(2,1)} %copy-done.6, ...), custom_call_target="tpu_custom_call" | custom-call | flops 75497472 | bytes 2097152 | tf_op jit(solution)/shard_map/pallas_call | solution.py:61
  58.0 5.3 %all-to-all-start.1 = ((bf16[4,16,24,384]{3,2,1,0:T(8,128)(2,1)}), bf16[4,16,24,384]{3,2,1,0:T(8,128)(2,1)S(1)}, u32[]{:S(2)}, u32[]{:S(2)}) async-start(bf16[4,16,24,384]{3,2,1,0:T(8,128)(2,1)} %get-tuple-element.24), calls=%async_computation.1 | async-start | bytes 2359296 | tf_op jit(solution)/shard_map/all_to_all | solution.py:401
  63.3 1.9 %collective-permute-start.2 = (bf16[1536,384]{1,0:T(8,128)(2,1)S(1)}, bf16[1536,384]{1,0:T(8,128)(2,1)S(1)}, u32[]{:S(2)}, u32[]{:S(2)}) collective-permute-start(bf16[1536,384]{1,0:T(8,128)(2,1)S(1)} %bitcast.18), channel_id=1, source_target_pairs={{0,2},{2,0},{1,3},{3,1},{4,6},{6,4},{5,7},{7,5},{8,10},{10,8},{9,1... | collective-permute-start | bytes 3538952 | tf_op jit(solution)/shard_map/ppermute | solution.py:50
  65.2 9.7 %all-to-all-done.1 = bf16[4,16,24,384]{3,2,1,0:T(8,128)(2,1)S(1)} async-done(((bf16[4,16,24,384]{3,2,1,0:T(8,128)(2,1)}), bf16[4,16,24,384]{3,2,1,0:T(8,128)(2,1)S(1)}, u32[]{:S(2)}, u32[]{:S(2)}) %all-to-all-start.1) | async-done | bytes 1179680 | tf_op jit(solution)/shard_map/all_to_all | solution.py:401
  74.9 1.9 %collective-permute-start.3 = (bf16[4,384,384]{2,1,0:T(8,128)(2,1)S(1)}, bf16[4,384,384]{2,1,0:T(8,128)(2,1)}, u32[]{:S(2)}, u32[]{:S(2)}) collective-permute-start(bf16[4,384,384]{2,1,0:T(8,128)(2,1)S(1)} %bitcast.23), channel_id=1, source_target_pairs={{0,2},{2,0},{1,3},{3,1},{4,6},{6,4},{5,7},{7,5},{8,10},{10,8},{9,1... | collective-permute-start | bytes 3538952 | tf_op jit(solution)/shard_map/ppermute | solution.py:50
  76.8 4.9 %all-to-all-start.3 = ((bf16[16,144,128]{2,1,0:T(8,128)(2,1)}), bf16[16,144,128]{2,1,0:T(8,128)(2,1)}, u32[]{:S(2)}, u32[]{:S(2)}) async-start(bf16[16,144,128]{2,1,0:T(8,128)(2,1)} %get-tuple-element.33), calls=%async_computation.3 | async-start | bytes 1179648 | tf_op jit(solution)/shard_map/all_to_all | solution.py:427
  84.3 2.2 %shard_map.110 = (f32[128,1408]{1,0:T(8,128)S(1)}, f32[8,128]{1,0:T(8,128)S(1)}) custom-call(bf16[128,384]{1,0:T(8,128)(2,1)S(1)} %get-tuple-element.22.hid_own, bf16[128,384]{1,0:T(8,128)(2,1)S(1)} %get-tuple-element.23.hid_other, bf16[4,384,384]{2,1,0:T(8,128)(2,1)S(1)} %bitcast.24, bf16[4,384,384]{2,1,0:T(8,128)(2,1)} %collective-permute-done.3.other, ...), custom_call_target="tpu_custom_call" | custom-call | flops 276824064 | bytes 4194304 | tf_op jit(solution)/shard_map/pallas_call | solution.py:61
  86.5 5.8 %all-gather.1 = f32[16,128]{1,0:T(8,128)S(1)} all-gather(f32[8,128]{1,0:T(8,128)S(1)} %get-tuple-element.27), channel_id=3, replica_groups=mesh['z'=16,'x'=4,'yl'=2,'c'=2,'yh'=2] {'yh'}, dimensions={0}, use_global_device_ids=true | all-gather | bytes 12288 | tf_op jit(solution)/shard_map/all_gather | solution.py:451
  92.4 2.3 %shard_map.111 = (f32[64,768]{1,0:T(8,128)S(1)}, bf16[64,768]{1,0:T(8,128)(2,1)S(1)}) custom-call(s32[1]{0:T(128)} %bitcast.3.yh_ref, f32[128,1408]{1,0:T(8,128)S(1)} %get-tuple-element.25.exp_s, f32[128,1408]{1,0:T(8,128)S(1)} %copy-done.1, f32[2,8,128]{2,1,0:T(8,128)S(1)} %bitcast.30, bf16[4,384,384]{2,1,0:T(8,128)(2,1)S(1)} %bitcast.25, ...), custom_call_target="tpu_custom_call" | custom-call | flops 276824064 | bytes 4194304 | tf_op jit(solution)/shard_map/pallas_call | solution.py:61
  94.7 3.1 %collective-permute-start.4 = (bf16[64,768]{1,0:T(8,128)(2,1)S(1)}, bf16[64,768]{1,0:T(8,128)(2,1)S(1)}, u32[]{:S(2)}, u32[]{:S(2)}) collective-permute-start(bf16[64,768]{1,0:T(8,128)(2,1)S(1)} %get-tuple-element.29), channel_id=1, source_target_pairs={{0,1},{1,0},{2,3},{3,2},{4,5},{5,4},{6,7},{7,6},{8,9},{9,8},{10,11... | collective-permute-start | bytes 294920 | tf_op jit(solution)/shard_map/ppermute | solution.py:50
  97.7 5.0 %collective-permute-done.4.received = bf16[64,768]{1,0:T(8,128)(2,1)S(1)} collective-permute-done((bf16[64,768]{1,0:T(8,128)(2,1)S(1)}, bf16[64,768]{1,0:T(8,128)(2,1)S(1)}, u32[]{:S(2)}, u32[]{:S(2)}) %collective-permute-start.4) | collective-permute-done | bytes 98336 | tf_op jit(solution)/shard_map/ppermute | solution.py:50
  103.8 5.8 %all-to-all-start.2 = ((bf16[8,64,384]{2,1,0:T(8,128)(2,1)}), bf16[8,64,384]{2,1,0:T(8,128)(2,1)S(1)}, u32[]{:S(2)}, u32[]{:S(2)}) async-start(bf16[8,64,384]{2,1,0:T(8,128)(2,1)} %get-tuple-element.31), calls=%async_computation.2 | async-start | bytes 786432 | tf_op jit(solution)/shard_map/all_to_all | solution.py:480
  110.9 5.5 %all-to-all-done.2.by_chip = bf16[8,64,384]{2,1,0:T(8,128)(2,1)S(1)} async-done(((bf16[8,64,384]{2,1,0:T(8,128)(2,1)}), bf16[8,64,384]{2,1,0:T(8,128)(2,1)S(1)}, u32[]{:S(2)}, u32[]{:S(2)}) %all-to-all-start.2) | async-done | bytes 393248 | tf_op jit(solution)/shard_map/all_to_all | solution.py:480
  116.4 2.4 %all_gather.25.everyone = bf16[1024,384]{1,0:T(8,128)(2,1)S(1)} all-gather(bf16[512,384]{1,0:T(8,128)(2,1)S(1)} %bitcast.28), channel_id=1, replica_groups=mesh['z'=16,'x'=4,'yl'=2,'c'=2,'yh'=2] {'c'}, dimensions={0}, use_global_device_ids=true | all-gather | bytes 1179648 | tf_op jit(solution)/shard_map/all_gather | solution.py:481
  119.8 9.2 %all-to-all-start.4 = ((bf16[16,16,384]{2,1,0:T(8,128)(2,1)}), bf16[16,16,384]{2,1,0:T(8,128)(2,1)S(1)}, u32[]{:S(2)}, u32[]{:S(2)}) async-start(bf16[16,16,384]{2,1,0:T(8,128)(2,1)} %shard_map.115), calls=%async_computation.4 | async-start | bytes 393216 | tf_op jit(solution)/shard_map/all_to_all | solution.py:493
  129.0 1.9 %shard_map.113 = f32[64,768]{1,0:T(8,128)S(1)} custom-call(s32[3]{0:T(128)S(1)} %pad_add_fusion.place, bf16[8,64,384]{2,1,0:T(8,128)(2,1)S(1)} %all-to-all-done.2.by_chip, f32[64,768]{1,0:T(8,128)S(1)} %get-tuple-element.32.hidden, bf16[1536,384]{1,0:T(8,128)(2,1)S(1)} %bitcast.22, bf16[1536,384]{1,0:T(8,128)(2,1)S(1)} %collective-permute-done.2.other), custom_call_target="tpu_custom_call" | custom-call | flops 75497472 | bytes 2097152 | tf_op jit(solution)/shard_map/pallas_call | solution.py:61
  131.0 2.8 %collective-permute-start.5 = (f32[64,768]{1,0:T(8,128)S(1)}, f32[64,768]{1,0:T(8,128)S(1)}, u32[]{:S(2)}, u32[]{:S(2)}) collective-permute-start(f32[64,768]{1,0:T(8,128)S(1)} %shard_map.113), channel_id=1, source_target_pairs={{0,1},{1,0},{2,3},{3,2},{4,5},{5,4},{6,7},{7,6},{8,9},{9,8},{10,11... | collective-permute-start | bytes 589832 | tf_op jit(solution)/shard_map/ppermute | solution.py:50
  133.8 7.0 %collective-permute-done.5 = f32[64,768]{1,0:T(8,128)S(1)} collective-permute-done((f32[64,768]{1,0:T(8,128)S(1)}, f32[64,768]{1,0:T(8,128)S(1)}, u32[]{:S(2)}, u32[]{:S(2)}) %collective-permute-start.5) | collective-permute-done | bytes 196640 | tf_op jit(solution)/shard_map/ppermute | solution.py:50
  141.5 3.6 %all-to-all-done.4 = bf16[16,16,384]{2,1,0:T(8,128)(2,1)S(1)} async-done(((bf16[16,16,384]{2,1,0:T(8,128)(2,1)}), bf16[16,16,384]{2,1,0:T(8,128)(2,1)S(1)}, u32[]{:S(2)}, u32[]{:S(2)}) %all-to-all-start.4) | async-done | bytes 196640 | tf_op jit(solution)/shard_map/all_to_all | solution.py:493
  145.2 6.0 %all-gather.3 = f32[2,9,384]{2,1,0:T(8,128)S(1)} all-gather(f32[1,9,384]{2,1,0:T(8,128)S(1)} %slice_bitcast_fusion), channel_id=4, replica_groups=mesh['z'=16,'x'=4,'yl'=2,'c'=2,'yh'=2] {'yh'}, dimensions={0}, use_global_device_ids=true | all-gather | bytes 41472 | tf_op jit(solution)/shard_map/all_gather | solution.py:495
  (35 shorter events, 12.8 us)
Async XLA Ops:
  38.9 1.3 copy-start
  40.2 4.8 %copy-start.5 = (bf16[1,128,768]{2,1,0:T(8,128)(2,1)S(1)}, bf16[1,128,768]{2,1,0:T(8,128)(2,1)}, u32[]{:S(2)}) copy-start(bf16[1,128,768]{2,1,0:T(8,128)(2,1)} %param.9) | copy-start | bytes 589828
  40.2 17.8 %all-to-all-start = ((bf16[4,16,24,384]{3,2,1,0:T(8,128)(2,1)}), bf16[4,16,24,384]{3,2,1,0:T(8,128)(2,1)S(1)}, u32[]{:S(2)}, u32[]{:S(2)}) async-start(bf16[4,16,24,384]{3,2,1,0:T(8,128)(2,1)} %shard_map.107), calls=%async_computation | async-start | bytes 2359296 | tf_op jit(solution)/shard_map/all_to_all | solution.py:351
  45.0 8.7 %collective-permute-start.1 = (bf16[128,768]{1,0:T(8,128)(2,1)S(1)}, bf16[128,768]{1,0:T(8,128)(2,1)S(1)}, u32[]{:S(2)}, u32[]{:S(2)}) collective-permute-start(bf16[128,768]{1,0:T(8,128)(2,1)S(1)} %bitcast.33), channel_id=1, source_target_pairs={{8,0},{16,8},{24,16},{9,1},{17,9},{25,17},{10,2},{18,10},{26,18},{... | collective-permute-start | bytes 589832 | tf_op jit(solution)/shard_map/ppermute | solution.py:46
  46.3 7.7 %collective-permute-start = (bf16[128,768]{1,0:T(8,128)(2,1)S(1)}, bf16[128,768]{1,0:T(8,128)(2,1)S(1)}, u32[]{:S(2)}, u32[]{:S(2)}) collective-permute-start(bf16[128,768]{1,0:T(8,128)(2,1)S(1)} %bitcast.34), channel_id=1, source_target_pairs={{0,8},{8,16},{16,24},{1,9},{9,17},{17,25},{2,10},{10,18},{18,26},{... | collective-permute-start | bytes 589832 | tf_op jit(solution)/shard_map/ppermute | solution.py:46
  53.7 0.7 copy-start.6
  54.0 0.7 copy-start.7
  58.0 16.9 %all-to-all-start.1 = ((bf16[4,16,24,384]{3,2,1,0:T(8,128)(2,1)}), bf16[4,16,24,384]{3,2,1,0:T(8,128)(2,1)S(1)}, u32[]{:S(2)}, u32[]{:S(2)}) async-start(bf16[4,16,24,384]{3,2,1,0:T(8,128)(2,1)} %get-tuple-element.24), calls=%async_computation.1 | async-start | bytes 2359296 | tf_op jit(solution)/shard_map/all_to_all | solution.py:401
  63.3 18.4 %collective-permute-start.2 = (bf16[1536,384]{1,0:T(8,128)(2,1)S(1)}, bf16[1536,384]{1,0:T(8,128)(2,1)S(1)}, u32[]{:S(2)}, u32[]{:S(2)}) collective-permute-start(bf16[1536,384]{1,0:T(8,128)(2,1)S(1)} %bitcast.18), channel_id=1, source_target_pairs={{0,2},{2,0},{1,3},{3,1},{4,6},{6,4},{5,7},{7,5},{8,10},{10,8},{9,1... | collective-permute-start | bytes 3538952 | tf_op jit(solution)/shard_map/ppermute | solution.py:50
  74.9 9.1 %collective-permute-start.3 = (bf16[4,384,384]{2,1,0:T(8,128)(2,1)S(1)}, bf16[4,384,384]{2,1,0:T(8,128)(2,1)}, u32[]{:S(2)}, u32[]{:S(2)}) collective-permute-start(bf16[4,384,384]{2,1,0:T(8,128)(2,1)S(1)} %bitcast.23), channel_id=1, source_target_pairs={{0,2},{2,0},{1,3},{3,1},{4,6},{6,4},{5,7},{7,5},{8,10},{10,8},{9,1... | collective-permute-start | bytes 3538952 | tf_op jit(solution)/shard_map/ppermute | solution.py:50
  76.8 27.0 %all-to-all-start.3 = ((bf16[16,144,128]{2,1,0:T(8,128)(2,1)}), bf16[16,144,128]{2,1,0:T(8,128)(2,1)}, u32[]{:S(2)}, u32[]{:S(2)}) async-start(bf16[16,144,128]{2,1,0:T(8,128)(2,1)} %get-tuple-element.33), calls=%async_computation.3 | async-start | bytes 1179648 | tf_op jit(solution)/shard_map/all_to_all | solution.py:427
  81.7 1.1 copy-start.2
  82.7 0.9 copy-start.3
  83.7 0.7 copy-start.4
  84.3 8.0 %copy-start.1 = (f32[128,1408]{1,0:T(8,128)S(1)}, f32[128,1408]{1,0:T(8,128)}, u32[]{:S(2)}) copy-start(f32[128,1408]{1,0:T(8,128)} %get-tuple-element.26.exp_t) | copy-start | bytes 2162692
  94.7 8.0 %collective-permute-start.4 = (bf16[64,768]{1,0:T(8,128)(2,1)S(1)}, bf16[64,768]{1,0:T(8,128)(2,1)S(1)}, u32[]{:S(2)}, u32[]{:S(2)}) collective-permute-start(bf16[64,768]{1,0:T(8,128)(2,1)S(1)} %get-tuple-element.29), channel_id=1, source_target_pairs={{0,1},{1,0},{2,3},{3,2},{4,5},{5,4},{6,7},{7,6},{8,9},{9,8},{10,11... | collective-permute-start | bytes 294920 | tf_op jit(solution)/shard_map/ppermute | solution.py:50
  103.8 12.6 %all-to-all-start.2 = ((bf16[8,64,384]{2,1,0:T(8,128)(2,1)}), bf16[8,64,384]{2,1,0:T(8,128)(2,1)S(1)}, u32[]{:S(2)}, u32[]{:S(2)}) async-start(bf16[8,64,384]{2,1,0:T(8,128)(2,1)} %get-tuple-element.31), calls=%async_computation.2 | async-start | bytes 786432 | tf_op jit(solution)/shard_map/all_to_all | solution.py:480
  119.8 25.4 %all-to-all-start.4 = ((bf16[16,16,384]{2,1,0:T(8,128)(2,1)}), bf16[16,16,384]{2,1,0:T(8,128)(2,1)S(1)}, u32[]{:S(2)}, u32[]{:S(2)}) async-start(bf16[16,16,384]{2,1,0:T(8,128)(2,1)} %shard_map.115), calls=%async_computation.4 | async-start | bytes 393216 | tf_op jit(solution)/shard_map/all_to_all | solution.py:493
  131.0 9.8 %collective-permute-start.5 = (f32[64,768]{1,0:T(8,128)S(1)}, f32[64,768]{1,0:T(8,128)S(1)}, u32[]{:S(2)}, u32[]{:S(2)}) collective-permute-start(f32[64,768]{1,0:T(8,128)S(1)} %shard_map.113), channel_id=1, source_target_pairs={{0,1},{1,0},{2,3},{3,2},{4,5},{5,4},{6,7},{7,6},{8,9},{9,8},{10,11... | collective-permute-start | bytes 589832 | tf_op jit(solution)/shard_map/ppermute | solution.py:50

commit v4 on v3

--- a/solution.py
+++ b/solution.py
@@ -247,7 +247,8 @@
     return jnp.transpose(jnp.concatenate([rows, jnp.zeros((count - rows.shape[0], count), F32)]))
 
 
-def head_kernel(hid_own, hid_other, own, other, target_stats, exp_ref, stats_ref):
+def head_kernel(hid_own, hid_other, own, other, target_stats, exp_ref, stats_ref, near_ref):
+    near_ref[...] = other[...]
     pos, tracks = exp_ref.shape
     wide = own.shape[2]
     for start in range(0, tracks, wide):
@@ -435,9 +436,9 @@
         owned,
     )
 
-    exp_s, stats = call(
+    exp_s, stats, head_near = call(
         head_kernel,
-        [SDS((pos, tracks), F32), SDS((8, pos), F32)],
+        [SDS((pos, tracks), F32), SDS((8, pos), F32), SDS(head_other.shape, BF)],
         [],
         2 * pos * width * tracks,
         4 * 1024 * 1024,
@@ -460,7 +461,7 @@
         exp_t,
         stats,
         head_own,
-        head_other,
+        head_near,
     )
     received = swapped(sent, "yh")
     copies, hidden_grad = call(

time: 153 us -> 152 us (level)
  transfers between devices with their start and end apart: 11 -> 11, of which waited for: 6 -> 6; matrix products, arithmetic and copies ran while one was open for 1% -> 1% of each run, Pallas kernels for 10% -> 9%
where the time goes in v4:
time: 152 us; the launch traced here: 151 us
  blocking collectives  50.8 us (33%)
  starting transfers between devices  45.3 us (30%)
  waiting for transfers between devices  31.2 us (21%)
  Pallas kernels  17.8 us (12%)
  local copies, waits for them, and re-layouts  2.53 us (2%)
    all_gather x1, blocking collectives, on_device(): gathered = lax.all_gather(packed, 'z', axis=0)  36.6 us
    pallas_call x12, Pallas kernels, call(): pl.pallas_call(body, out_shape=outs, in_specs=specs, out_specs=[spec(k, f...  17.8 us
    ppermute x4, waiting for transfers between devices, swapped(): return lax.ppermute(value, axis, [(0, 1), (1, 0)])  12 us
    all_to_all x1, waiting for transfers between devices, on_device(): head_own = lax.all_to_all(head_copies, 'x', 0, 0).reshape(4, zc * slab, ch)  9.68 us
    ppermute x4, starting transfers between devices, swapped(): return lax.ppermute(value, axis, [(0, 1), (1, 0)])  9.57 us
    all_to_all x1, starting transfers between devices, on_device(): terms = lax.all_to_all(kernel_part, 'z', 0, 0)  9.15 us
    all_gather x1, blocking collectives, on_device(): kernel_pair = lax.all_gather(kernel_sum, 'yh', axis=0)  6.01 us
    all_gather x1, blocking collectives, on_device(): stats = lax.all_gather(stats, 'yh', axis=0)  5.85 us
  transfers between devices with their start and end apart: 11, of which 6 were waited for; matrix products, arithmetic and copies ran while one was open for 1% of the time, Pallas kernels for 9%

profile of v4, /device:TPU:56, one launch (start us, length us, event | category | flops | bytes accessed | tf_op | source)
XLA Modules:
  0.0 150.6 jit_solution(12553031798969273366)
XLA Ops:
  0.6 1.6 %shard_map.104 = bf16[2,24,384]{2,1,0:T(8,128)(2,1)} custom-call(bf16[144,384]{1,0:T(8,128)(2,1)} %conv_far.1, bf16[24,768]{1,0:T(8,128)(2,1)} %proj_far.1, bf16[48,1408]{1,0:T(8,128)(2,1)} %head_far.1), custom_call_target="tpu_custom_call" | custom-call | flops 14155776 | bytes 524288 | tf_op jit(solution)/shard_map/pallas_call | solution.py:61
  2.3 36.6 %all-gather = bf16[32,24,384]{2,1,0:T(8,128)(2,1)S(1)} all-gather(bf16[2,24,384]{2,1,0:T(8,128)(2,1)} %shard_map.104), channel_id=2, replica_groups=mesh['z'=16,'x'=4,'yl'=2,'c'=2,'yh'=2] {'z'}, dimensions={0}, use_global_device_ids=true | all-gather | bytes 626688 | tf_op jit(solution)/shard_map/all_gather | solution.py:348
  40.2 4.8 %all-to-all-start = ((bf16[4,16,24,384]{3,2,1,0:T(8,128)(2,1)}), bf16[4,16,24,384]{3,2,1,0:T(8,128)(2,1)S(1)}, u32[]{:S(2)}, u32[]{:S(2)}) async-start(bf16[4,16,24,384]{3,2,1,0:T(8,128)(2,1)} %shard_map.107), calls=%async_computation | async-start | bytes 2359296 | tf_op jit(solution)/shard_map/all_to_all | solution.py:352
  46.3 4.6 %collective-permute-start = (bf16[128,768]{1,0:T(8,128)(2,1)S(1)}, bf16[128,768]{1,0:T(8,128)(2,1)S(1)}, u32[]{:S(2)}, u32[]{:S(2)}) collective-permute-start(bf16[128,768]{1,0:T(8,128)(2,1)S(1)} %bitcast.34), channel_id=1, source_target_pairs={{0,8},{8,16},{16,24},{1,9},{9,17},{17,25},{2,10},{10,18},{18,26},{... | collective-permute-start | bytes 589832 | tf_op jit(solution)/shard_map/ppermute | solution.py:46
  51.5 2.2 %shard_map.105 = (f32[128,1408]{1,0:T(8,128)}, f32[2,128]{1,0:T(2,128)}) custom-call(s32[1]{0:T(128)S(6)} %copy.11.member, bf16[128,1408]{1,0:T(8,128)(2,1)} %bitcast.31, f32[4,1408]{1,0:T(4,128)} %member_bias.1, s32[1408]{0:T(1024)} %assay.1, f32[1,4]{1,0:T(1,128)} %bitcast.36), custom_call_target="tpu_custom_call" | custom-call | flops 720896 | bytes 1572864 | tf_op jit(solution)/shard_map/pallas_call | solution.py:61
  54.7 3.3 %shard_map.106 = (bf16[2,128,1152]{2,1,0:T(8,128)(2,1)}, bf16[2,128,384]{2,1,0:T(8,128)(2,1)}, bf16[16,144,128]{2,1,0:T(8,128)(2,1)}, bf16[4,16,24,384]{3,2,1,0:T(8,128)(2,1)}) custom-call(s32[1]{0:T(128)} %bitcast.core_ref, bf16[128,768]{1,0:T(8,128)(2,1)} %copy-done.7, bf16[128,768]{1,0:T(8,128)(2,1)} %bitcast.32, bf16[128,768]{1,0:T(8,128)(2,1)} %copy-done.6, ...), custom_call_target="tpu_custom_call" | custom-call | flops 75497472 | bytes 2097152 | tf_op jit(solution)/shard_map/pallas_call | solution.py:61
  58.0 5.3 %all-to-all-start.1 = ((bf16[4,16,24,384]{3,2,1,0:T(8,128)(2,1)}), bf16[4,16,24,384]{3,2,1,0:T(8,128)(2,1)S(1)}, u32[]{:S(2)}, u32[]{:S(2)}) async-start(bf16[4,16,24,384]{3,2,1,0:T(8,128)(2,1)} %get-tuple-element.25), calls=%async_computation.1 | async-start | bytes 2359296 | tf_op jit(solution)/shard_map/all_to_all | solution.py:402
  63.3 1.9 %collective-permute-start.2 = (bf16[1536,384]{1,0:T(8,128)(2,1)S(1)}, bf16[1536,384]{1,0:T(8,128)(2,1)S(1)}, u32[]{:S(2)}, u32[]{:S(2)}) collective-permute-start(bf16[1536,384]{1,0:T(8,128)(2,1)S(1)} %bitcast.18), channel_id=1, source_target_pairs={{0,2},{2,0},{1,3},{3,1},{4,6},{6,4},{5,7},{7,5},{8,10},{10,8},{9,1... | collective-permute-start | bytes 3538952 | tf_op jit(solution)/shard_map/ppermute | solution.py:50
  65.2 9.7 %all-to-all-done.1 = bf16[4,16,24,384]{3,2,1,0:T(8,128)(2,1)S(1)} async-done(((bf16[4,16,24,384]{3,2,1,0:T(8,128)(2,1)}), bf16[4,16,24,384]{3,2,1,0:T(8,128)(2,1)S(1)}, u32[]{:S(2)}, u32[]{:S(2)}) %all-to-all-start.1) | async-done | bytes 1179680 | tf_op jit(solution)/shard_map/all_to_all | solution.py:402
  74.9 1.9 %collective-permute-start.3 = (bf16[4,384,384]{2,1,0:T(8,128)(2,1)S(1)}, bf16[4,384,384]{2,1,0:T(8,128)(2,1)}, u32[]{:S(2)}, u32[]{:S(2)}) collective-permute-start(bf16[4,384,384]{2,1,0:T(8,128)(2,1)S(1)} %bitcast.23), channel_id=1, source_target_pairs={{0,2},{2,0},{1,3},{3,1},{4,6},{6,4},{5,7},{7,5},{8,10},{10,8},{9,1... | collective-permute-start | bytes 3538952 | tf_op jit(solution)/shard_map/ppermute | solution.py:50
  76.8 4.9 %all-to-all-start.3 = ((bf16[16,144,128]{2,1,0:T(8,128)(2,1)}), bf16[16,144,128]{2,1,0:T(8,128)(2,1)}, u32[]{:S(2)}, u32[]{:S(2)}) async-start(bf16[16,144,128]{2,1,0:T(8,128)(2,1)} %get-tuple-element.35), calls=%async_computation.3 | async-start | bytes 1179648 | tf_op jit(solution)/shard_map/all_to_all | solution.py:428
  84.3 2.3 %shard_map.110 = (f32[128,1408]{1,0:T(8,128)S(1)}, f32[8,128]{1,0:T(8,128)S(1)}, bf16[4,384,384]{2,1,0:T(8,128)(2,1)S(1)}) custom-call(bf16[128,384]{1,0:T(8,128)(2,1)S(1)} %get-tuple-element.23.hid_own, bf16[128,384]{1,0:T(8,128)(2,1)S(1)} %get-tuple-element.24.hid_other, bf16[4,384,384]{2,1,0:T(8,128)(2,1)S(1)} %bitcast.24, ...), custom_call_target="tpu_custom_call" | custom-call | flops 276824064 | bytes 4194304 | tf_op jit(solution)/shard_map/pallas_call | solution.py:61
  86.6 5.8 %all-gather.1 = f32[16,128]{1,0:T(8,128)S(1)} all-gather(f32[8,128]{1,0:T(8,128)S(1)} %get-tuple-element.28), channel_id=3, replica_groups=mesh['z'=16,'x'=4,'yl'=2,'c'=2,'yh'=2] {'yh'}, dimensions={0}, use_global_device_ids=true | all-gather | bytes 12288 | tf_op jit(solution)/shard_map/all_gather | solution.py:452
  93.5 3.1 %collective-permute-start.4 = (bf16[64,768]{1,0:T(8,128)(2,1)S(1)}, bf16[64,768]{1,0:T(8,128)(2,1)S(1)}, u32[]{:S(2)}, u32[]{:S(2)}) collective-permute-start(bf16[64,768]{1,0:T(8,128)(2,1)S(1)} %get-tuple-element.31), channel_id=1, source_target_pairs={{0,1},{1,0},{2,3},{3,2},{4,5},{5,4},{6,7},{7,6},{8,9},{9,8},{10,11... | collective-permute-start | bytes 294920 | tf_op jit(solution)/shard_map/ppermute | solution.py:50
  96.6 4.9 %collective-permute-done.4.received = bf16[64,768]{1,0:T(8,128)(2,1)S(1)} collective-permute-done((bf16[64,768]{1,0:T(8,128)(2,1)S(1)}, bf16[64,768]{1,0:T(8,128)(2,1)S(1)}, u32[]{:S(2)}, u32[]{:S(2)}) %collective-permute-start.4) | collective-permute-done | bytes 98336 | tf_op jit(solution)/shard_map/ppermute | solution.py:50
  102.6 5.8 %all-to-all-start.2 = ((bf16[8,64,384]{2,1,0:T(8,128)(2,1)}), bf16[8,64,384]{2,1,0:T(8,128)(2,1)S(1)}, u32[]{:S(2)}, u32[]{:S(2)}) async-start(bf16[8,64,384]{2,1,0:T(8,128)(2,1)} %get-tuple-element.33), calls=%async_computation.2 | async-start | bytes 786432 | tf_op jit(solution)/shard_map/all_to_all | solution.py:481
  109.7 5.5 %all-to-all-done.2.by_chip = bf16[8,64,384]{2,1,0:T(8,128)(2,1)S(1)} async-done(((bf16[8,64,384]{2,1,0:T(8,128)(2,1)}), bf16[8,64,384]{2,1,0:T(8,128)(2,1)S(1)}, u32[]{:S(2)}, u32[]{:S(2)}) %all-to-all-start.2) | async-done | bytes 393248 | tf_op jit(solution)/shard_map/all_to_all | solution.py:481
  115.2 2.4 %all_gather.25.everyone = bf16[1024,384]{1,0:T(8,128)(2,1)S(1)} all-gather(bf16[512,384]{1,0:T(8,128)(2,1)S(1)} %bitcast.28), channel_id=1, replica_groups=mesh['z'=16,'x'=4,'yl'=2,'c'=2,'yh'=2] {'c'}, dimensions={0}, use_global_device_ids=true | all-gather | bytes 1179648 | tf_op jit(solution)/shard_map/all_gather | solution.py:482
  118.6 9.2 %all-to-all-start.4 = ((bf16[16,16,384]{2,1,0:T(8,128)(2,1)}), bf16[16,16,384]{2,1,0:T(8,128)(2,1)S(1)}, u32[]{:S(2)}, u32[]{:S(2)}) async-start(bf16[16,16,384]{2,1,0:T(8,128)(2,1)} %shard_map.115), calls=%async_computation.4 | async-start | bytes 393216 | tf_op jit(solution)/shard_map/all_to_all | solution.py:494
  127.8 1.9 %shard_map.113 = f32[64,768]{1,0:T(8,128)S(1)} custom-call(s32[3]{0:T(128)S(1)} %pad_add_fusion.place, bf16[8,64,384]{2,1,0:T(8,128)(2,1)S(1)} %all-to-all-done.2.by_chip, f32[64,768]{1,0:T(8,128)S(1)} %get-tuple-element.34.hidden, bf16[1536,384]{1,0:T(8,128)(2,1)S(1)} %bitcast.22, bf16[1536,384]{1,0:T(8,128)(2,1)S(1)} %collective-permute-done.2.other), custom_call_target="tpu_custom_call" | custom-call | flops 75497472 | bytes 2097152 | tf_op jit(solution)/shard_map/pallas_call | solution.py:61
  129.8 2.7 %collective-permute-start.5 = (f32[64,768]{1,0:T(8,128)S(1)}, f32[64,768]{1,0:T(8,128)S(1)}, u32[]{:S(2)}, u32[]{:S(2)}) collective-permute-start(f32[64,768]{1,0:T(8,128)S(1)} %shard_map.113), channel_id=1, source_target_pairs={{0,1},{1,0},{2,3},{3,2},{4,5},{5,4},{6,7},{7,6},{8,9},{9,8},{10,11... | collective-permute-start | bytes 589832 | tf_op jit(solution)/shard_map/ppermute | solution.py:50
  132.5 7.1 %collective-permute-done.5 = f32[64,768]{1,0:T(8,128)S(1)} collective-permute-done((f32[64,768]{1,0:T(8,128)S(1)}, f32[64,768]{1,0:T(8,128)S(1)}, u32[]{:S(2)}, u32[]{:S(2)}) %collective-permute-start.5) | collective-permute-done | bytes 196640 | tf_op jit(solution)/shard_map/ppermute | solution.py:50
  140.3 3.6 %all-to-all-done.4 = bf16[16,16,384]{2,1,0:T(8,128)(2,1)S(1)} async-done(((bf16[16,16,384]{2,1,0:T(8,128)(2,1)}), bf16[16,16,384]{2,1,0:T(8,128)(2,1)S(1)}, u32[]{:S(2)}, u32[]{:S(2)}) %all-to-all-start.4) | async-done | bytes 196640 | tf_op jit(solution)/shard_map/all_to_all | solution.py:494
  144.0 6.0 %all-gather.3 = f32[2,9,384]{2,1,0:T(8,128)S(1)} all-gather(f32[1,9,384]{2,1,0:T(8,128)S(1)} %slice_bitcast_fusion), channel_id=4, replica_groups=mesh['z'=16,'x'=4,'yl'=2,'c'=2,'yh'=2] {'yh'}, dimensions={0}, use_global_device_ids=true | all-gather | bytes 41472 | tf_op jit(solution)/shard_map/all_gather | solution.py:496
  (35 shorter events, 12.2 us)
Async XLA Ops:
  38.9 1.3 copy-start
  40.2 4.8 %copy-start.5 = (bf16[1,128,768]{2,1,0:T(8,128)(2,1)S(1)}, bf16[1,128,768]{2,1,0:T(8,128)(2,1)}, u32[]{:S(2)}) copy-start(bf16[1,128,768]{2,1,0:T(8,128)(2,1)} %param.9) | copy-start | bytes 589828
  40.2 17.8 %all-to-all-start = ((bf16[4,16,24,384]{3,2,1,0:T(8,128)(2,1)}), bf16[4,16,24,384]{3,2,1,0:T(8,128)(2,1)S(1)}, u32[]{:S(2)}, u32[]{:S(2)}) async-start(bf16[4,16,24,384]{3,2,1,0:T(8,128)(2,1)} %shard_map.107), calls=%async_computation | async-start | bytes 2359296 | tf_op jit(solution)/shard_map/all_to_all | solution.py:352
  45.0 8.7 %collective-permute-start.1 = (bf16[128,768]{1,0:T(8,128)(2,1)S(1)}, bf16[128,768]{1,0:T(8,128)(2,1)S(1)}, u32[]{:S(2)}, u32[]{:S(2)}) collective-permute-start(bf16[128,768]{1,0:T(8,128)(2,1)S(1)} %bitcast.33), channel_id=1, source_target_pairs={{8,0},{16,8},{24,16},{9,1},{17,9},{25,17},{10,2},{18,10},{26,18},{... | collective-permute-start | bytes 589832 | tf_op jit(solution)/shard_map/ppermute | solution.py:46
  46.3 7.7 %collective-permute-start = (bf16[128,768]{1,0:T(8,128)(2,1)S(1)}, bf16[128,768]{1,0:T(8,128)(2,1)S(1)}, u32[]{:S(2)}, u32[]{:S(2)}) collective-permute-start(bf16[128,768]{1,0:T(8,128)(2,1)S(1)} %bitcast.34), channel_id=1, source_target_pairs={{0,8},{8,16},{16,24},{1,9},{9,17},{17,25},{2,10},{10,18},{18,26},{... | collective-permute-start | bytes 589832 | tf_op jit(solution)/shard_map/ppermute | solution.py:46
  53.7 0.7 copy-start.6
  54.0 0.7 copy-start.7
  58.0 16.9 %all-to-all-start.1 = ((bf16[4,16,24,384]{3,2,1,0:T(8,128)(2,1)}), bf16[4,16,24,384]{3,2,1,0:T(8,128)(2,1)S(1)}, u32[]{:S(2)}, u32[]{:S(2)}) async-start(bf16[4,16,24,384]{3,2,1,0:T(8,128)(2,1)} %get-tuple-element.25), calls=%async_computation.1 | async-start | bytes 2359296 | tf_op jit(solution)/shard_map/all_to_all | solution.py:402
  63.3 18.4 %collective-permute-start.2 = (bf16[1536,384]{1,0:T(8,128)(2,1)S(1)}, bf16[1536,384]{1,0:T(8,128)(2,1)S(1)}, u32[]{:S(2)}, u32[]{:S(2)}) collective-permute-start(bf16[1536,384]{1,0:T(8,128)(2,1)S(1)} %bitcast.18), channel_id=1, source_target_pairs={{0,2},{2,0},{1,3},{3,1},{4,6},{6,4},{5,7},{7,5},{8,10},{10,8},{9,1... | collective-permute-start | bytes 3538952 | tf_op jit(solution)/shard_map/ppermute | solution.py:50
  74.9 9.1 %collective-permute-start.3 = (bf16[4,384,384]{2,1,0:T(8,128)(2,1)S(1)}, bf16[4,384,384]{2,1,0:T(8,128)(2,1)}, u32[]{:S(2)}, u32[]{:S(2)}) collective-permute-start(bf16[4,384,384]{2,1,0:T(8,128)(2,1)S(1)} %bitcast.23), channel_id=1, source_target_pairs={{0,2},{2,0},{1,3},{3,1},{4,6},{6,4},{5,7},{7,5},{8,10},{10,8},{9,1... | collective-permute-start | bytes 3538952 | tf_op jit(solution)/shard_map/ppermute | solution.py:50
  76.8 25.8 %all-to-all-start.3 = ((bf16[16,144,128]{2,1,0:T(8,128)(2,1)}), bf16[16,144,128]{2,1,0:T(8,128)(2,1)}, u32[]{:S(2)}, u32[]{:S(2)}) async-start(bf16[16,144,128]{2,1,0:T(8,128)(2,1)} %get-tuple-element.35), calls=%async_computation.3 | async-start | bytes 1179648 | tf_op jit(solution)/shard_map/all_to_all | solution.py:428
  81.7 1.1 copy-start.2
  82.7 0.9 copy-start.3
  83.7 0.7 copy-start.4
  84.3 8.1 %copy-start.1 = (f32[128,1408]{1,0:T(8,128)S(1)}, f32[128,1408]{1,0:T(8,128)}, u32[]{:S(2)}) copy-start(f32[128,1408]{1,0:T(8,128)} %get-tuple-element.27.exp_t) | copy-start | bytes 2162692
  93.5 8.0 %collective-permute-start.4 = (bf16[64,768]{1,0:T(8,128)(2,1)S(1)}, bf16[64,768]{1,0:T(8,128)(2,1)S(1)}, u32[]{:S(2)}, u32[]{:S(2)}) collective-permute-start(bf16[64,768]{1,0:T(8,128)(2,1)S(1)} %get-tuple-element.31), channel_id=1, source_target_pairs={{0,1},{1,0},{2,3},{3,2},{4,5},{5,4},{6,7},{7,6},{8,9},{9,8},{10,11... | collective-permute-start | bytes 294920 | tf_op jit(solution)/shard_map/ppermute | solution.py:50
  102.6 12.6 %all-to-all-start.2 = ((bf16[8,64,384]{2,1,0:T(8,128)(2,1)}), bf16[8,64,384]{2,1,0:T(8,128)(2,1)S(1)}, u32[]{:S(2)}, u32[]{:S(2)}) async-start(bf16[8,64,384]{2,1,0:T(8,128)(2,1)} %get-tuple-element.33), calls=%async_computation.2 | async-start | bytes 786432 | tf_op jit(solution)/shard_map/all_to_all | solution.py:481
  118.6 25.4 %all-to-all-start.4 = ((bf16[16,16,384]{2,1,0:T(8,128)(2,1)}), bf16[16,16,384]{2,1,0:T(8,128)(2,1)S(1)}, u32[]{:S(2)}, u32[]{:S(2)}) async-start(bf16[16,16,384]{2,1,0:T(8,128)(2,1)} %shard_map.115), calls=%async_computation.4 | async-start | bytes 393216 | tf_op jit(solution)/shard_map/all_to_all | solution.py:494
  129.8 9.8 %collective-permute-start.5 = (f32[64,768]{1,0:T(8,128)S(1)}, f32[64,768]{1,0:T(8,128)S(1)}, u32[]{:S(2)}, u32[]{:S(2)}) collective-permute-start(f32[64,768]{1,0:T(8,128)S(1)} %shard_map.113), channel_id=1, source_target_pairs={{0,1},{1,0},{2,3},{3,2},{4,5},{5,4},{6,7},{7,6},{8,9},{9,8},{10,11... | collective-permute-start | bytes 589832 | tf_op jit(solution)/shard_map/ppermute | solution.py:50
